TPU v7x, 32 devices: a whole 2x2x4 slice. The times are simulated.
32 devices in a mesh: grid: 2 (over core), img: 16 (over z, y, x).
Axes of the slice: x: 2, y: 2, z: 4, core: 2. Of those that a mesh axis runs over, the one named last changes fastest.
Arguments:
- images: bfloat16 [128, 24, 24, 384], P('img', 'grid'), may hold values from -6 to 6
- cotangent: bfloat16 [128, 24, 24, 384], P('img', 'grid'), may hold values from -6 to 6
- image_group: int32 [128], P('img'), may hold values from 0 to 1
- row_order: int32 [2, 24], replicated, may hold values from 0 to 23, each once within a row
- keep_mask: int32 [128, 2, 2], P('img'), may hold values 0 or 1
- resample: float32 [2, 24, 13, 112], P(None, 'grid'), may hold values from -0.5 to 0.5
- filters: float32 [2, 112, 2, 384], P(None, None, None, 'img'), may hold values from -4.2 to 4.2
- filters_first: float32 [2, 112, 2, 384], P(None, None, None, 'img')
- filters_second: float32 [2, 112, 2, 384], P(None, None, None, 'img')
- expand: float32 [2, 384, 1536], P(None, 'img'), may hold values from -0.3125 to 0.3125
- expand_first: float32 [2, 384, 1536], P(None, 'img')
- expand_second: float32 [2, 384, 1536], P(None, 'img')
- shrink: float32 [2, 1536, 384], P(None, 'img'), may hold values from -0.25 to 0.25
- shrink_first: float32 [2, 1536, 384], P(None, 'img')
- shrink_second: float32 [2, 1536, 384], P(None, 'img')
- norm_params: float32 [2, 4, 384], P(None, None, 'img')
- norm_first: float32 [2, 4, 384], P(None, None, 'img')
- norm_second: float32 [2, 4, 384], P(None, None, 'img')
- mlp_bias: float32 [2, 1920], P(None, 'img'), may hold values from -1.8 to 1.8
- bias_first: float32 [2, 1920], P(None, 'img')
- bias_second: float32 [2, 1920], P(None, 'img')
Outputs:
- output: bfloat16 [128, 24, 24, 384], P('img', 'grid')
- image_grad: float32 [128, 24, 24, 384], P('img', 'grid')
- new_filters: float32 [2, 112, 2, 384], P(None, None, None, 'img')
- new_filters_first: float32 [2, 112, 2, 384], P(None, None, None, 'img')
- new_filters_second: float32 [2, 112, 2, 384], P(None, None, None, 'img')
- new_expand: float32 [2, 384, 1536], P(None, 'img')
- new_expand_first: float32 [2, 384, 1536], P(None, 'img')
- new_expand_second: float32 [2, 384, 1536], P(None, 'img')
- new_shrink: float32 [2, 1536, 384], P(None, 'img')
- new_shrink_first: float32 [2, 1536, 384], P(None, 'img')
- new_shrink_second: float32 [2, 1536, 384], P(None, 'img')
- new_norms: float32 [2, 4, 384], P(None, None, 'img')
- new_norm_first: float32 [2, 4, 384], P(None, None, 'img')
- new_norm_second: float32 [2, 4, 384], P(None, None, 'img')
- new_bias: float32 [2, 1920], P(None, 'img')
- new_bias_first: float32 [2, 1920], P(None, 'img')
- new_bias_second: float32 [2, 1920], P(None, 'img')
Inputs may be any that keep to these rules, and one draw needn't show every extreme that they name: `row_order`: each row is a permutation of the 24 row slots.
All inputs are finite; a program needn't handle non-finite values. No bound on the sum of `keep_mask` on one device may be relied on, other than what follows from the above.
Results may differ from a plain program's by a relative error of at most 0.025.
Values may be sent and summed in bfloat16 or wider, within the bound.
A program may use at most 256 MiB of HBM per device.

v0:
```python
import math

import jax
import jax.numpy as jnp
from jax import lax
from jax.sharding import PartitionSpec as P

SIDE = 24
SIDE_LOW = 14
HALF = 13
BASE = 112
LAYERS = 2
STEP = 10


NORM_EPS = 1e-06
DROP_RATES = (0.1, 0.15)
BETA_ONE = 0.9
BETA_TWO = 0.999
ADAM_EPS = 1e-08
LEARN_RATES = (0.5, 0.04, 0.02, 0.3, 0.2)
WEIGHT_DECAYS = (0.05, 0.05, 0.05, 0.0, 0.0)
HIGHEST = lax.Precision.HIGHEST


def phase_tables(slot_rows, height):
    freq_rows = jnp.arange(SIDE, dtype=jnp.int32)[:, None, None, None]
    freq_cols = jnp.arange(HALF, dtype=jnp.int32)[None, :, None, None]
    image_rows = slot_rows[None, None, :, None]
    columns = jnp.arange(SIDE, dtype=jnp.int32)[None, None, None, :]
    phase_count = (freq_rows * image_rows + freq_cols * columns) % height
    angles = phase_count.astype(jnp.float32) * (2.0 * math.pi / height)
    live_mask = (
        (freq_rows < height)
        & (freq_cols <= height // 2)
        & (image_rows < height)
        & (columns < height)
    )
    live_value = live_mask.astype(jnp.float32)
    forward = jnp.stack([jnp.cos(angles) * live_value, -jnp.sin(angles) * live_value], axis=2)
    edge_cols = (freq_cols == 0) | (freq_cols == height // 2)
    col_weight = jnp.where(edge_cols, 1.0, 2.0).astype(jnp.float32) / (height * height)
    inverse = forward * col_weight[:, :, None, :, :]
    slot_count = slot_rows.shape[0]
    return (
        forward.reshape(2 * SIDE * HALF, slot_count * SIDE),
        inverse.reshape(2 * SIDE * HALF, slot_count * SIDE),
    )


def layer_norm(values, gain, shift):
    mean_value = jnp.mean(values, axis=-1, keepdims=True)
    centred = values - mean_value
    variance = jnp.mean(centred * centred, axis=-1, keepdims=True)
    inv_std = lax.rsqrt(variance + NORM_EPS)
    normal = centred * inv_std
    return (normal * gain + shift, normal, inv_std)


def norm_back(grad_out, normal, inv_std, gain):
    scaled = grad_out * gain
    grad_in = inv_std * (
        scaled
        - jnp.mean(scaled, axis=-1, keepdims=True)
        - normal * jnp.mean(scaled * normal, axis=-1, keepdims=True)
    )
    return (grad_in, jnp.sum(grad_out * normal, axis=(0, 1)), jnp.sum(grad_out, axis=(0, 1)))


def gelu_exact(values):
    return jax.nn.gelu(values, approximate=False)


def adamw(weight, first, second, grad, rate, decay):
    first_new = BETA_ONE * first + (1.0 - BETA_ONE) * grad
    second_new = BETA_TWO * second + (1.0 - BETA_TWO) * grad * grad
    first_hat = first_new / (1.0 - BETA_ONE**STEP)
    second_hat = second_new / (1.0 - BETA_TWO**STEP)
    weight_new = weight - rate * (first_hat / (jnp.sqrt(second_hat) + ADAM_EPS) + decay * weight)
    return (weight_new, first_new, second_new)


def choose_group(image_group, pair):
    return jnp.where((image_group == 1)[:, None, None], pair[1][None], pair[0][None])


def body(
    images,
    cotangent,
    image_group,
    row_order,
    keep_mask,
    resample,
    filters,
    filters_first,
    filters_second,
    expand,
    expand_first,
    expand_second,
    shrink,
    shrink_first,
    shrink_second,
    norm_params,
    norm_first,
    norm_second,
    mlp_bias,
    bias_first,
    bias_second,
):
    count_img = images.shape[0]
    row_slots = images.shape[1]
    width = images.shape[3]
    local_tok = row_slots * SIDE
    half_local = resample.shape[1] * HALF
    spec_local = half_local * 2
    grid_index = lax.axis_index("grid")
    filt_all, expand_all, shrink_all, norm_all, bias_all = (
        lax.all_gather(filters.astype(jnp.bfloat16), "img", axis=3, tiled=True),
        lax.all_gather(expand.astype(jnp.bfloat16), "img", axis=1, tiled=True),
        lax.all_gather(shrink.astype(jnp.bfloat16), "img", axis=1, tiled=True),
        lax.all_gather(norm_params.astype(jnp.bfloat16), "img", axis=2, tiled=True),
        lax.all_gather(mlp_bias.astype(jnp.bfloat16), "img", axis=1, tiled=True),
    )
    hidden_units = expand_all.shape[2]
    heights = (SIDE_LOW, SIDE)
    fwd_list = []
    inv_list = []
    for group_id in range(2):
        slot_rows = lax.dynamic_slice_in_dim(row_order[group_id], grid_index * row_slots, row_slots)
        fwd_tab, inv_tab = phase_tables(slot_rows, heights[group_id])
        fwd_list.append(fwd_tab)
        inv_list.append(inv_tab)
    token_fwd = choose_group(image_group, jnp.stack(fwd_list).astype(jnp.bfloat16))
    token_inv = choose_group(image_group, jnp.stack(inv_list).astype(jnp.bfloat16))
    local_map = resample.reshape(2, half_local, BASE)
    selector = (image_group == 1)[None, None, :, None]
    member = jnp.stack([image_group == 0, image_group == 1], axis=1).astype(jnp.float32)
    rate_scale = jnp.array(
        [1.0 / (1.0 - DROP_RATES[0]), 1.0 / (1.0 - DROP_RATES[1])], dtype=jnp.float32
    )
    keep_scale = keep_mask.astype(jnp.float32) * rate_scale[None, :, None]
    norm_values = norm_all.astype(jnp.float32)
    bias_values = bias_all.astype(jnp.float32)
    residual = images.astype(jnp.float32).reshape(count_img, local_tok, width)
    saved = []
    for layer_id in range(LAYERS):
        normed_a, normal_a, inv_a = layer_norm(
            residual, norm_values[layer_id, 0], norm_values[layer_id, 1]
        )
        normed_a_low = normed_a.astype(jnp.bfloat16)
        spec = (
            lax.psum_scatter(
                jnp.einsum(
                    "ist,itd->sid", token_fwd, normed_a_low, preferred_element_type=jnp.float32
                ).astype(jnp.bfloat16),
                "grid",
                scatter_dimension=0,
                tiled=True,
            )
            .astype(jnp.float32)
            .reshape(half_local, 2, count_img, width)
        )
        filt_loc = jnp.einsum(
            "gsj,jqd->gsqd", local_map, filt_all[layer_id].astype(jnp.float32), precision=HIGHEST
        )
        filt_img = jnp.where(selector, filt_loc[1][:, :, None, :], filt_loc[0][:, :, None, :])
        real_part = spec[:, 0] * filt_img[:, 0] - spec[:, 1] * filt_img[:, 1]
        imag_part = spec[:, 0] * filt_img[:, 1] + spec[:, 1] * filt_img[:, 0]
        mixed_spec = (
            jnp.stack([real_part, imag_part], axis=1)
            .reshape(spec_local, count_img, width)
            .astype(jnp.bfloat16)
        )
        mixer = jnp.einsum(
            "ist,sid->itd",
            token_inv,
            lax.all_gather(mixed_spec, "grid", axis=0, tiled=True),
            preferred_element_type=jnp.float32,
        )
        mixer_scale = keep_scale[:, layer_id, 0][:, None, None]
        middle = residual + mixer_scale * mixer
        normed_b, normal_b, inv_b = layer_norm(
            middle, norm_values[layer_id, 2], norm_values[layer_id, 3]
        )
        normed_b_low = normed_b.astype(jnp.bfloat16)
        pre = (
            jnp.einsum(
                "itd,df->itf",
                normed_b_low,
                expand_all[layer_id],
                preferred_element_type=jnp.float32,
            )
            + bias_values[layer_id, :hidden_units]
        )
        act_low = gelu_exact(pre).astype(jnp.bfloat16)
        branch = (
            jnp.einsum(
                "itf,fd->itd", act_low, shrink_all[layer_id], preferred_element_type=jnp.float32
            )
            + bias_values[layer_id, hidden_units:]
        )
        mlp_scale = keep_scale[:, layer_id, 1][:, None, None]
        residual = middle + mlp_scale * branch
        saved.append(
            (
                normal_a,
                inv_a,
                normed_a_low,
                spec,
                filt_img,
                normal_b,
                inv_b,
                normed_b_low,
                pre,
                act_low,
            )
        )
    output = residual.astype(jnp.bfloat16).reshape(count_img, row_slots, SIDE, width)
    grad_up = cotangent.astype(jnp.float32).reshape(count_img, local_tok, width)
    grad_filters = [None] * LAYERS
    grad_expand = [None] * LAYERS
    grad_shrink = [None] * LAYERS
    grad_norms = [None] * LAYERS
    grad_bias = [None] * LAYERS
    for layer_id in range(LAYERS - 1, -1, -1):
        (
            normal_a,
            inv_a,
            normed_a_low,
            spec,
            filt_img,
            normal_b,
            inv_b,
            normed_b_low,
            pre,
            act_low,
        ) = saved[layer_id]
        mixer_scale = keep_scale[:, layer_id, 0][:, None, None]
        mlp_scale = keep_scale[:, layer_id, 1][:, None, None]
        grad_branch = (grad_up * mlp_scale).astype(jnp.bfloat16)
        grad_shrink[layer_id] = jnp.einsum(
            "itf,itd->fd", act_low, grad_branch, preferred_element_type=jnp.float32
        )
        bias_out = jnp.sum(grad_branch, axis=(0, 1), dtype=jnp.float32)
        d_act = jnp.einsum(
            "itd,fd->itf", grad_branch, shrink_all[layer_id], preferred_element_type=jnp.float32
        )
        gelu_pull = jax.vjp(gelu_exact, pre)[1]
        d_pre_low = gelu_pull(d_act)[0].astype(jnp.bfloat16)
        grad_expand[layer_id] = jnp.einsum(
            "itd,itf->df", normed_b_low, d_pre_low, preferred_element_type=jnp.float32
        )
        bias_hidden = jnp.sum(d_pre_low, axis=(0, 1), dtype=jnp.float32)
        d_normed_b = jnp.einsum(
            "itf,df->itd", d_pre_low, expand_all[layer_id], preferred_element_type=jnp.float32
        )
        d_middle, gain_b_grad, shift_b_grad = norm_back(
            d_normed_b, normal_b, inv_b, norm_values[layer_id, 2]
        )
        grad_mid = grad_up + d_middle
        grad_mixer = (grad_mid * mixer_scale).astype(jnp.bfloat16)
        d_mixed = (
            lax.psum_scatter(
                jnp.einsum(
                    "ist,itd->sid", token_inv, grad_mixer, preferred_element_type=jnp.float32
                ).astype(jnp.bfloat16),
                "grid",
                scatter_dimension=0,
                tiled=True,
            )
            .astype(jnp.float32)
            .reshape(half_local, 2, count_img, width)
        )
        d_real = d_mixed[:, 0]
        d_imag = d_mixed[:, 1]
        prod_real = d_real * spec[:, 0] + d_imag * spec[:, 1]
        prod_imag = d_imag * spec[:, 0] - d_real * spec[:, 1]
        group_terms = jnp.einsum(
            "ig,sqid->gsqd", member, jnp.stack([prod_real, prod_imag], axis=1), precision=HIGHEST
        )
        grad_filters[layer_id] = jnp.einsum(
            "gsj,gsqd->jqd", local_map, group_terms, precision=HIGHEST
        )
        spec_real = d_real * filt_img[:, 0] + d_imag * filt_img[:, 1]
        spec_imag = d_imag * filt_img[:, 0] - d_real * filt_img[:, 1]
        d_spec_low = (
            jnp.stack([spec_real, spec_imag], axis=1)
            .reshape(spec_local, count_img, width)
            .astype(jnp.bfloat16)
        )
        d_normed_a = jnp.einsum(
            "ist,sid->itd",
            token_fwd,
            lax.all_gather(d_spec_low, "grid", axis=0, tiled=True),
            preferred_element_type=jnp.float32,
        )
        d_input, gain_a_grad, shift_a_grad = norm_back(
            d_normed_a, normal_a, inv_a, norm_values[layer_id, 0]
        )
        grad_up = grad_mid + d_input
        grad_norms[layer_id] = jnp.stack(
            [gain_a_grad, shift_a_grad, gain_b_grad, shift_b_grad], axis=0
        )
        grad_bias[layer_id] = jnp.concatenate([bias_hidden, bias_out], axis=0)
    image_grad = grad_up.reshape(count_img, row_slots, SIDE, width)
    full_filters = jnp.stack(grad_filters)
    full_expand = jnp.stack(grad_expand)
    full_shrink = jnp.stack(grad_shrink)
    full_norms = jnp.stack(grad_norms)
    full_bias = jnp.stack(grad_bias)
    total_filters, total_expand, total_shrink, total_norms, total_bias = (
        lax.psum(full_filters.astype(jnp.bfloat16), "grid").astype(jnp.float32),
        lax.psum(full_expand.astype(jnp.bfloat16), "grid").astype(jnp.float32),
        lax.psum(full_shrink.astype(jnp.bfloat16), "grid").astype(jnp.float32),
        lax.psum(full_norms.astype(jnp.bfloat16), "grid").astype(jnp.float32),
        lax.psum(full_bias.astype(jnp.bfloat16), "grid").astype(jnp.float32),
    )
    summed = (
        lax.psum_scatter(
            total_filters.astype(jnp.bfloat16), "img", scatter_dimension=3, tiled=True
        ).astype(jnp.float32),
        lax.psum_scatter(
            total_expand.astype(jnp.bfloat16), "img", scatter_dimension=1, tiled=True
        ).astype(jnp.float32),
        lax.psum_scatter(
            total_shrink.astype(jnp.bfloat16), "img", scatter_dimension=1, tiled=True
        ).astype(jnp.float32),
        lax.psum_scatter(
            total_norms.astype(jnp.bfloat16), "img", scatter_dimension=2, tiled=True
        ).astype(jnp.float32),
        lax.psum_scatter(
            total_bias.astype(jnp.bfloat16), "img", scatter_dimension=1, tiled=True
        ).astype(jnp.float32),
    )
    weights = (filters, expand, shrink, norm_params, mlp_bias)
    firsts = (filters_first, expand_first, shrink_first, norm_first, bias_first)
    seconds = (filters_second, expand_second, shrink_second, norm_second, bias_second)
    updated = []
    for index in range(5):
        updated.extend(
            adamw(
                weights[index],
                firsts[index],
                seconds[index],
                summed[index],
                LEARN_RATES[index],
                WEIGHT_DECAYS[index],
            )
        )
    return (
        output,
        image_grad,
        updated[0],
        updated[1],
        updated[2],
        updated[3],
        updated[4],
        updated[5],
        updated[6],
        updated[7],
        updated[8],
        updated[9],
        updated[10],
        updated[11],
        updated[12],
        updated[13],
        updated[14],
    )


def solution(mesh):
    return jax.shard_map(
        body,
        mesh=mesh,
        in_specs=(
            P("img", "grid", None, None),
            P("img", "grid", None, None),
            P("img"),
            P(),
            P("img", None, None),
            P(None, "grid", None, None),
            P(None, None, None, "img"),
            P(None, None, None, "img"),
            P(None, None, None, "img"),
            P(None, "img", None),
            P(None, "img", None),
            P(None, "img", None),
            P(None, "img", None),
            P(None, "img", None),
            P(None, "img", None),
            P(None, None, "img"),
            P(None, None, "img"),
            P(None, None, "img"),
            P(None, "img"),
            P(None, "img"),
            P(None, "img"),
        ),
        out_specs=(
            P("img", "grid", None, None),
            P("img", "grid", None, None),
            P(None, None, None, "img"),
            P(None, None, None, "img"),
            P(None, None, None, "img"),
            P(None, "img", None),
            P(None, "img", None),
            P(None, "img", None),
            P(None, "img", None),
            P(None, "img", None),
            P(None, "img", None),
            P(None, None, "img"),
            P(None, None, "img"),
            P(None, None, "img"),
            P(None, "img"),
            P(None, "img"),
            P(None, "img"),
        ),
        check_vma=False,
    )
```

profile of v0, /device:TPU:0, one launch (start us, length us, event | category | flops | bytes accessed | tf_op | source)
XLA Modules:
  0.0 1053.8 jit_solution(4837836608213772870)
XLA Ops:
  9.2 3.0 multiply_reduce_fusion.11
  12.8 23.0 %and_select_fusion.3 = (f32[24,13,1,12,24]{4,3,2,1,0:T(8,128)S(1)}, f32[24,13,1,12,24]{4,3,2,1,0:T(8,128)S(1)}, f32[24,13,1,12,24]{4,3,2,1,0:T(8,128)S(1)}, f32[24,13,1,12,24]{4,3,2,1,0:T(8,128)}) fusion(s32[13,24]{1,0:T(8,128)S(1)} %iota_multiply_fusion.2, s32[24,12]{1,0:T(8,128)S(1)} %iota_multiply_fusion.1, pred[24]{0:T(512)(128)(4,1)S(1)} %get-tuple-element.218, ...), kind=kLoop, calls=%fused_computation.115 | loop fusion | flops 2336256 | bytes 1448784 | tf_op jit(solution)/shard_map/mul | solution.py:40
  35.8 2.9 pad_maximum_fusion
  38.6 4.1 stack.162
  45.7 2.0 copy.149
  47.6 4.7 pad_maximum_fusion.1
  52.3 4.1 stack.164
  59.7 43.6 %all_gather.27 = bf16[2,4,384]{1,0,2:T(2,128)(2,1)S(1)} all-gather(bf16[2,4,24]{1,0,2:T(2,128)(2,1)S(1)} %copy.148), channel_id=1, replica_groups=mesh['grid'=2,'img'=16] {'img'}, dimensions={2}, use_global_device_ids=true | all-gather | bytes 6528 | tf_op jit(solution)/shard_map/all_gather | solution.py:121
  103.4 11.2 %slice_reduce_fusion.1 = (f32[384]{0:T(512)}, f32[384]{0:T(512)}, f32[384]{0:T(512)}, f32[384]{0:T(512)}, f32[384]{0:T(512)S(1)}, /*index=5*/f32[384]{0:T(512)S(1)}, f32[384]{0:T(512)S(1)}, f32[384]{0:T(512)S(1)}) fusion(f32[2,4,384]{1,0,2:T(2,128)S(1)} %convert_element_type.202), kind=kLoop, calls=%fused_computation.241 | loop fusion | bytes 24576 | tf_op jit(solution)/shard_map/slice | solution.py:183
  114.8 4.4 convert_bitcast_fusion.3
  119.2 2.6 copy.208
  122.7 38.1 %all_gather.28 = bf16[2,112,2,384]{1,2,0,3:T(2,128)(2,1)S(1)} all-gather(bf16[2,112,2,24]{1,2,0,3:T(2,128)(2,1)S(1)} %copy.235), channel_id=1, replica_groups=mesh['grid'=2,'img'=16] {'img'}, dimensions={3}, use_global_device_ids=true | all-gather | bytes 365568 | tf_op jit(solution)/shard_map/all_gather | solution.py:118
  164.9 3.6 broadcast_select_fusion
  171.0 2.3 copy-done
  177.3 37.2 %all-gather = bf16[16,120,2]{1,2,0:T(2,128)(2,1)S(1)} all-gather(bf16[1,120,2]{1,2,0:T(2,128)(2,1)S(1)} %convert_bitcast_fusion.6), channel_id=1, replica_groups=mesh['grid'=2,'img'=16] {'img'}, dimensions={0}, use_global_device_ids=true | all-gather | bytes 8160 | tf_op jit(solution)/shard_map/all_gather | solution.py:122
  217.0 4.2 fusion.160
  223.9 29.7 %all-gather.10.cloned.1.call-done = bf16[2,384,1536]{2,1,0:T(8,128)(2,1)} async-done(((bf16[2,24,1536]{2,1,0:T(8,128)(2,1)}), bf16[2,384,1536]{2,1,0:T(8,128)(2,1)}) %all-gather.10.cloned.1.call-update) | async-done | bytes 2359312 | tf_op jit(solution)/shard_map/all_gather | solution.py:119
  253.6 9.9 fusion.40
  263.5 5.1 copy-done.16
  268.6 34.9 %multiply_convert_fusion.1 = (bf16[8,288,1536]{2,1,0:T(8,128)(2,1)}, f32[8,288,1536]{2,1,0:T(8,128)}) fusion(f32[8,288,1536]{2,1,0:T(8,128)S(1)} %get-tuple-element.199, f32[1536]{0:T(1024)} %copy-done.63, u8[288,1536]{1,0:T(8,128)(4,1)S(1)} %get-tuple-element.88, u8[288,1536]{1,0:T(8,128)(4,1)S(1)} %get-tuple-element.87), kind=kLoop, calls=%fused_computation.28 | loop fusion | flops 251265024 | bytes 36280320 | tf_op jit(solution)/shard_map/convert_element_type | solution.py:195
  303.5 14.4 %all-gather.12.cloned.1.call-done = bf16[2,1536,384]{2,1,0:T(8,128)(2,1)} async-done(((bf16[2,96,384]{2,1,0:T(8,128)(2,1)}), bf16[2,1536,384]{2,1,0:T(8,128)(2,1)}) %all-gather.12.cloned.1.call-update) | async-done | bytes 2359312 | tf_op jit(solution)/shard_map/all_gather | solution.py:120
  317.9 6.7 fusion.161
  326.3 3.5 convert_bitcast_fusion.2
  329.9 2.6 copy.209
  332.5 10.7 %reduce-scatter.23.cloned.1.call-done = bf16[312,3072]{1,0:T(8,128)(2,1)} async-done(((bf16[624,3072]{1,0:T(8,128)(2,1)}), bf16[312,3072]{1,0:T(8,128)(2,1)}) %reduce-scatter.23.cloned.1.call-update) | async-done | bytes 1916944
  345.7 2.3 copy-done.2
  350.7 4.0 fusion.154
  354.7 10.2 all-gather.14.cloned.1.call-done
  364.9 5.5 fusion.162
  371.3 2.0 copy-done.110
  373.4 7.8 fusion.41
  381.3 34.3 %multiply_convert_fusion = (bf16[8,288,1536]{2,1,0:T(8,128)(2,1)}, f32[8,288,1536]{2,1,0:T(8,128)}) fusion(f32[8,288,1536]{2,1,0:T(8,128)S(1)} %get-tuple-element.204, f32[1536]{0:T(1024)S(1)} %copy-done.65, u8[288,1536]{1,0:T(8,128)(4,1)S(1)} %get-tuple-element.86, u8[288,1536]{1,0:T(8,128)(4,1)S(1)} %get-tuple-element.85), kind=kLoop, calls=%fused_computation.15 | loop fusion | flops 251265024 | bytes 36280320 | tf_op jit(solution)/shard_map/convert_element_type | solution.py:195
  415.6 17.1 %fusion.163 = (bf16[1536]{0:T(1024)(128)(2,1)}, bf16[8,288,1536]{2,1,0:T(8,128)(2,1)}) fusion(f32[8,288,1536]{2,1,0:T(8,128)} %get-tuple-element.145, bf16[8,288,384]{2,1,0:T(8,128)(2,1)S(1)} %bitcast.262, bf16[2,1536,384]{2,1,0:T(8,128)(2,1)} %all-gather.12.cloned.1.call-done, f32[8,288,1536]{2,1,0:T(8,128)} %copy-done.17, f32[1536]{0:T(1024)S(1)} %copy-done.65), kind=kOutput, calls=%fused_computation.342 | convolution fusion | flops 2774530560 | bytes 38347776 | tf_op jit(solution)/shard_map/itd,fd->itf/dot_general | solution.py:245
  432.7 8.2 multiply_reduce_fusion
  441.0 2.7 fusion.37
  443.7 3.1 convert_bitcast_fusion.1
  446.8 2.6 copy.210
  449.5 13.0 %reduce-scatter.25.cloned.1.call-done = bf16[312,3072]{1,0:T(8,128)(2,1)} async-done(((bf16[624,3072]{1,0:T(8,128)(2,1)}), bf16[312,3072]{1,0:T(8,128)(2,1)}) %reduce-scatter.25.cloned.1.call-update) | async-done | bytes 1916944
  467.6 3.0 multiply_add_fusion.6
  472.5 8.3 fusion.56
  480.8 5.9 all-gather.16.cloned.1.call-done
  486.8 6.7 multiply_reduce_fusion.1
  493.6 3.6 fusion.153
  497.2 18.2 %fusion.164 = (bf16[1536]{0:T(1024)(128)(2,1)}, bf16[8,288,1536]{2,1,0:T(8,128)(2,1)}) fusion(f32[8,288,1536]{2,1,0:T(8,128)} %get-tuple-element.147, bf16[8,288,384]{2,1,0:T(8,128)(2,1)S(1)} %get-tuple-element.140, bf16[2,1536,384]{2,1,0:T(8,128)(2,1)S(1)} %copy-done.109, f32[8,288,1536]{2,1,0:T(8,128)} %copy-done.16, f32[1536]{0:T(1024)S(1)} %copy-done.64), kind=kOutput, calls=%fused_computation.343 | convolution fusion | flops 2774530560 | bytes 38349824 | tf_op jit(solution)/shard_map/itd,fd->itf/dot_general | solution.py:245
  515.5 6.2 fusion.57
  521.9 2.4 copy.196
  526.5 7.5 fusion.54
  534.0 7.0 fusion.55
  542.8 8.2 multiply_reduce_fusion.2
  552.9 3.0 convert_bitcast_fusion
  555.9 2.6 copy.211
  560.1 3.4 fusion.32
  564.4 91.6 %reduce-scatter.29.cloned.1.call-done = bf16[24,3072]{1,0:T(8,128)(2,1)} async-done(((bf16[384,3072]{1,0:T(8,128)(2,1)}), bf16[24,3072]{1,0:T(8,128)(2,1)}) %reduce-scatter.29.cloned.1.call-update) | async-done | bytes 147472
  657.7 131.5 %reduce-scatter.19.cloned.1.call-done = bf16[2,96,384]{2,1,0:T(8,128)(2,1)} async-done(((bf16[2,1536,384]{2,1,0:T(8,128)(2,1)}), bf16[2,96,384]{2,1,0:T(8,128)(2,1)}) %reduce-scatter.19.cloned.1.call-update) | async-done | bytes 147472 | tf_op jit(solution)/shard_map/reduce_scatter | solution.py:325
  789.3 13.1 %reduce-scatter.27.cloned.1.call-done = bf16[312,3072]{1,0:T(8,128)(2,1)} async-done(((bf16[624,3072]{1,0:T(8,128)(2,1)}), bf16[312,3072]{1,0:T(8,128)(2,1)}) %reduce-scatter.27.cloned.1.call-update) | async-done | bytes 1916944
  818.8 8.4 add_convert_fusion.2
  827.5 2.4 multiply_subtract_fusion.2
  829.9 2.3 multiply_subtract_fusion.3
  832.2 106.7 %all-reduce.9.cloned.1.call-done = bf16[2,112,2,384]{1,2,0,3:T(2,128)(2,1)} async-done(((bf16[2,112,2,384]{1,2,0,3:T(2,128)(2,1)}), bf16[2,112,2,384]{1,2,0,3:T(2,128)(2,1)}) %all-reduce.9.cloned.1.call-update) | async-done | bytes 344080
  939.8 12.8 %all-gather.18.cloned.1.call-done = bf16[624,8,384]{2,0,1:T(8,128)(2,1)} async-done(((bf16[312,8,384]{2,0,1:T(8,128)(2,1)}), bf16[624,8,384]{2,0,1:T(8,128)(2,1)}) %all-gather.18.cloned.1.call-update) | async-done | bytes 3833872 | tf_op jit(solution)/shard_map/all_gather | solution.py:294
  952.6 5.7 multiply_reduce_fusion.3
  958.4 77.0 %all-reduce.3 = (bf16[2,4,384]{2,1,0:T(4,128)(2,1)S(1)}, bf16[2,1920]{1,0:T(2,128)(2,1)S(1)}) all-reduce(bf16[2,4,384]{2,1,0:T(4,128)(2,1)S(1)} %pad_maximum_fusion.10, bf16[2,1920]{1,0:T(2,128)(2,1)S(1)} %pad_maximum_fusion.9), channel_id=9, replica_groups=mesh['grid'=2,'img'=16] {'img'}, use_global_device_ids=true, to_apply=%region_35.36.clone | all-reduce | flops 6912 | bytes 27648
  1035.6 3.4 all-reduce.4
  1040.9 6.2 multiply_add_fusion
  (372 shorter events, 68.1 us)
Async XLA Ops:
  7.2 161.3 %reduce-scatter.21.cloned.1.call-start = ((), (), s32[]{:S(2)}) async-start(), calls=%async_computation.13 | async-start | bytes 5750784
  12.3 102.5 %copy-start.51 = (f32[8,288]{1,0:T(8,128)}, f32[8,288]{1,0:T(8,128)S(1)}, u32[]{:S(2)}) copy-start(f32[8,288]{1,0:T(8,128)S(1)} %div.134) | copy-start | bytes 27652
  52.3 7.2 copy-start.66
  56.5 58.1 %copy-start.45 = (f32[8,12,24]{2,1,0:T(8,128)S(1)}, f32[8,12,24]{2,1,0:T(8,128)}, u32[]{:S(2)}) copy-start(f32[8,12,24]{2,1,0:T(8,128)} %multiply_reduce_fusion.11) | copy-start | bytes 27652
  56.5 58.3 %copy-start.8 = (bf16[8,12,24,384]{3,2,1,0:T(8,128)(2,1)S(1)}, bf16[8,12,24,384]{3,2,1,0:T(8,128)(2,1)}, u32[]{:S(2)}) copy-start(bf16[8,12,24,384]{3,2,1,0:T(8,128)(2,1)} %param.22) | copy-start | bytes 5308420
  58.9 60.3 %copy-start.36 = (bf16[624,288]{0,1:T(8,128)(2,1)}, bf16[624,288]{0,1:T(8,128)(2,1)S(1)}, u32[]{:S(2)}) copy-start(bf16[624,288]{0,1:T(8,128)(2,1)S(1)} %copy.150) | copy-start | bytes 1078276
  59.5 157.5 %copy-start.87 = (pred[8]{0:T(512)(128)(4,1)}, pred[8]{0:T(512)(128)(4,1)S(1)}, u32[]{:S(2)}) copy-start(pred[8]{0:T(512)(128)(4,1)S(1)} %get-tuple-element.194) | copy-start | bytes 28
  114.6 138.9 %copy-start.83 = (f32[384]{0:T(512)}, f32[384]{0:T(512)S(1)}, u32[]{:S(2)}) copy-start(f32[384]{0:T(512)S(1)} %get-tuple-element.109) | copy-start | bytes 4612
  121.8 39.3 %copy-start.24 = (f32[2,12,13,112]{3,0,2,1:T(2,128)S(1)}, f32[2,12,13,112]{3,0,2,1:T(2,128)}, u32[]{:S(2)}) copy-start(f32[2,12,13,112]{3,0,2,1:T(2,128)} %param.27) | copy-start | bytes 419332
  121.9 95.2 %all-gather.8.cloned.1.call-start = ((), (), s32[]{:S(2)}) async-start(), calls=%async_computation.6 | async-start | bytes 5750784 | tf_op jit(solution)/shard_map/all_gather | solution.py:177
  174.1 41.7 %copy-start.26 = (bf16[624,288]{1,0:T(8,128)(2,1)S(1)}, bf16[624,288]{1,0:T(8,128)(2,1)}, u32[]{:S(2)}) copy-start(bf16[624,288]{1,0:T(8,128)(2,1)} %get-tuple-element.174) | copy-start | bytes 1078276
  174.2 42.1 %copy-start.94 = (s32[8,2,2]{0,2,1:T(2,128)S(1)}, s32[8,2,2]{0,2,1:T(2,128)}, u32[]{:S(2)}) copy-start(s32[8,2,2]{0,2,1:T(2,128)} %param.26) | copy-start | bytes 388
  174.2 42.1 %copy-start.104 = (f32[2]{0:T(128)S(1)}, f32[2]{0:T(128)}, u32[]{:S(2)}) copy-start(f32[2]{0:T(128)} %constant.212.clone) | copy-start | bytes 28
  175.7 77.9 %all-gather.10.cloned.1.call-start = ((), (), s32[]{:S(2)}) async-start(), calls=%async_computation.7 | async-start | bytes 2506752 | tf_op jit(solution)/shard_map/all_gather | solution.py:119
  176.5 141.5 %all-gather.12.cloned.1.call-start = ((), (), s32[]{:S(2)}) async-start(), calls=%async_computation.8 | async-start | bytes 2506752 | tf_op jit(solution)/shard_map/all_gather | solution.py:120
  177.2 165.9 %reduce-scatter.23.cloned.1.call-start = ((), (), s32[]{:S(2)}) async-start(), calls=%async_computation.14 | async-start | bytes 5750784
  215.2 38.4 %copy-start.63 = (f32[1536]{0:T(1024)}, f32[1536]{0:T(1024)S(1)}, u32[]{:S(2)}) copy-start(f32[1536]{0:T(1024)S(1)} %get-tuple-element.116) | copy-start | bytes 18436
  223.9 39.6 %copy-start.55 = (f32[8,288]{1,0:T(8,128)}, f32[8,288]{1,0:T(8,128)S(1)}, u32[]{:S(2)}) copy-start(f32[8,288]{1,0:T(8,128)S(1)} %add_rsqrt_fusion.3) | copy-start | bytes 27652
  268.6 49.4 %copy-start.11 = (f32[8,288,384]{2,1,0:T(8,128)S(1)}, f32[8,288,384]{2,1,0:T(8,128)}, u32[]{:S(2)}) copy-start(f32[8,288,384]{2,1,0:T(8,128)} %copy-done.10) | copy-start | bytes 10616836
  332.5 32.4 %all-gather.14.cloned.1.call-start = ((), (), s32[]{:S(2)}) async-start(), calls=%async_computation.9 | async-start | bytes 5750784 | tf_op jit(solution)/shard_map/all_gather | solution.py:177
  350.4 112.1 %reduce-scatter.25.cloned.1.call-start = ((), (), s32[]{:S(2)}) async-start(), calls=%async_computation.15 | async-start | bytes 5750784
  370.4 70.5 %copy-start.18 = (f32[8,288,384]{2,1,0:T(8,128)}, f32[8,288,384]{2,1,0:T(8,128)S(1)}, u32[]{:S(2)}) copy-start(f32[8,288,384]{2,1,0:T(8,128)S(1)} %get-tuple-element.203) | copy-start | bytes 10616836
  370.4 70.5 %copy-start.50 = (f32[8,288]{1,0:T(8,128)}, f32[8,288]{1,0:T(8,128)S(1)}, u32[]{:S(2)}) copy-start(f32[8,288]{1,0:T(8,128)S(1)} %broadcast_multiply_fusion.9) | copy-start | bytes 27652
  371.3 69.6 %copy-start.62 = (f32[8,288]{1,0:T(8,128)}, f32[8,288]{1,0:T(8,128)S(1)}, u32[]{:S(2)}) copy-start(f32[8,288]{1,0:T(8,128)S(1)} %add_rsqrt_fusion.1) | copy-start | bytes 27652
  381.2 34.3 %copy-start.17 = (f32[8,288,1536]{2,1,0:T(8,128)}, f32[8,288,1536]{2,1,0:T(8,128)S(1)}, u32[]{:S(2)}) copy-start(f32[8,288,1536]{2,1,0:T(8,128)S(1)} %get-tuple-element.204) | copy-start | bytes 42467332
  381.3 34.3 %copy-start.30 = (bf16[8,12,24,384]{3,2,1,0:T(8,128)(2,1)S(1)}, bf16[8,12,24,384]{3,2,1,0:T(8,128)(2,1)}, u32[]{:S(2)}) copy-start(bf16[8,12,24,384]{3,2,1,0:T(8,128)(2,1)} %get-tuple-element.143) | copy-start | bytes 5308420
  432.7 8.2 copy-start.23
  432.7 8.2 copy-start.73
  449.5 37.3 %all-gather.16.cloned.1.call-start = ((), (), s32[]{:S(2)}) async-start(), calls=%async_computation.10 | async-start | bytes 5750784 | tf_op jit(solution)/shard_map/all_gather | solution.py:294
  472.3 183.7 %reduce-scatter.29.cloned.1.call-start = ((), (), s32[]{:S(2)}) async-start(), calls=%async_computation.17 | async-start | bytes 2506752
  486.8 6.8 copy-start.92
  497.2 18.3 %copy-start.28 = (bf16[8,288,384]{2,1,0:T(8,128)(2,1)}, bf16[8,288,384]{2,1,0:T(8,128)(2,1)S(1)}, u32[]{:S(2)}) copy-start(bf16[8,288,384]{2,1,0:T(8,128)(2,1)S(1)} %get-tuple-element.140) | copy-start | bytes 5308420
  497.2 18.2 %copy-start.56 = (f32[8,288]{1,0:T(8,128)S(1)}, f32[8,288]{1,0:T(8,128)}, u32[]{:S(2)}) copy-start(f32[8,288]{1,0:T(8,128)} %copy-done.55) | copy-start | bytes 27652
  497.2 18.2 %copy-start.84 = (f32[384]{0:T(512)S(1)}, f32[384]{0:T(512)}, u32[]{:S(2)}) copy-start(f32[384]{0:T(512)} %copy-done.83) | copy-start | bytes 4612
  526.2 263.0 %reduce-scatter.19.cloned.1.call-start = ((), (), s32[]{:S(2)}) async-start(), calls=%async_computation.12 | async-start | bytes 2506752 | tf_op jit(solution)/shard_map/reduce_scatter | solution.py:325
  526.5 7.5 copy-start.29
  542.7 259.6 %reduce-scatter.27.cloned.1.call-start = ((), (), s32[]{:S(2)}) async-start(), calls=%async_computation.16 | async-start | bytes 5750784
  542.8 8.3 copy-start.15
  542.8 8.3 copy-start.57
  558.6 268.9 %all-reduce.11.cloned.1.call-start = ((), (), s32[]{:S(2)}) async-start(), calls=%async_computation.19 | async-start | bytes 589824 | tf_op jit(solution)/shard_map/psum | solution.py:313
  789.2 149.7 %all-reduce.9.cloned.1.call-start = ((), (), s32[]{:S(2)}) async-start(), calls=%async_computation.18 | async-start | bytes 786432
  812.5 140.1 %all-gather.18.cloned.1.call-start = ((), (), s32[]{:S(2)}) async-start(), calls=%async_computation.11 | async-start | bytes 5750784 | tf_op jit(solution)/shard_map/all_gather | solution.py:294
  818.7 8.6 copy-start.78
  818.7 8.6 copy-start.80
  818.8 8.6 copy-start.99
  818.8 8.6 copy-start.98
  818.8 8.6 copy-start.97
  818.8 8.6 copy-start.96
  827.2 125.4 %copy-start.9 = (bf16[8,12,24,384]{3,2,1,0:T(8,128)(2,1)S(1)}, bf16[8,12,24,384]{3,2,1,0:T(8,128)(2,1)}, u32[]{:S(2)}) copy-start(bf16[8,12,24,384]{3,2,1,0:T(8,128)(2,1)} %param.22) | copy-start | bytes 5308420
  827.2 125.4 %copy-start.35 = (bf16[624,288]{0,1:T(8,128)(2,1)S(1)}, bf16[624,288]{0,1:T(8,128)(2,1)}, u32[]{:S(2)}) copy-start(bf16[624,288]{0,1:T(8,128)(2,1)} %copy.149) | copy-start | bytes 1078276
  827.3 125.4 %copy-start.38 = (bf16[624,288]{0,1:T(8,128)(2,1)S(1)}, bf16[624,288]{0,1:T(8,128)(2,1)}, u32[]{:S(2)}) copy-start(bf16[624,288]{0,1:T(8,128)(2,1)} %copy-done.36) | copy-start | bytes 1078276
  827.3 125.4 %copy-start.52 = (f32[8,288]{1,0:T(8,128)S(1)}, f32[8,288]{1,0:T(8,128)}, u32[]{:S(2)}) copy-start(f32[8,288]{1,0:T(8,128)} %copy-done.51) | copy-start | bytes 27652
  827.3 125.4 %copy-start.54 = (f32[8,288]{1,0:T(8,128)S(1)}, f32[8,288]{1,0:T(8,128)}, u32[]{:S(2)}) copy-start(f32[8,288]{1,0:T(8,128)} %copy-done.53) | copy-start | bytes 27652
  827.3 125.4 %copy-start.69 = (f32[384]{0:T(512)S(1)}, f32[384]{0:T(512)}, u32[]{:S(2)}) copy-start(f32[384]{0:T(512)} %copy-done.68) | copy-start | bytes 4612
  827.3 125.4 %copy-start.91 = (pred[8]{0:T(512)(128)(4,1)S(1)}, pred[8]{0:T(512)(128)(4,1)}, u32[]{:S(2)}) copy-start(pred[8]{0:T(512)(128)(4,1)} %copy-done.87) | copy-start | bytes 28
  939.7 99.3 %copy-start.47 = (f32[2,112,2,24]{1,3,2,0:T(8,128)S(1)}, f32[2,112,2,24]{1,3,2,0:T(8,128)}, u32[]{:S(2)}) copy-start(f32[2,112,2,24]{1,3,2,0:T(8,128)} %param.28) | copy-start | bytes 129028
  939.7 99.3 %copy-start.60 = (f32[2,112,2,24]{1,3,2,0:T(8,128)S(1)}, f32[2,112,2,24]{1,3,2,0:T(8,128)}, u32[]{:S(2)}) copy-start(f32[2,112,2,24]{1,3,2,0:T(8,128)} %param.29) | copy-start | bytes 129028
  939.7 99.3 %copy-start.61 = (f32[2,112,2,24]{1,3,2,0:T(8,128)S(1)}, f32[2,112,2,24]{1,3,2,0:T(8,128)}, u32[]{:S(2)}) copy-start(f32[2,112,2,24]{1,3,2,0:T(8,128)} %param.30) | copy-start | bytes 129028
  939.7 100.0 %copy-start.67 = (f32[2,4,24]{2,1,0:T(4,128)S(1)}, f32[2,4,24]{2,1,0:T(4,128)}, u32[]{:S(2)}) copy-start(f32[2,4,24]{2,1,0:T(4,128)} %param.37) | copy-start | bytes 2308
  939.7 100.0 %copy-start.81 = (f32[2,4,24]{2,1,0:T(4,128)S(1)}, f32[2,4,24]{2,1,0:T(4,128)}, u32[]{:S(2)}) copy-start(f32[2,4,24]{2,1,0:T(4,128)} %param.38) | copy-start | bytes 2308
  939.7 100.0 %copy-start.82 = (f32[2,4,24]{2,1,0:T(4,128)S(1)}, f32[2,4,24]{2,1,0:T(4,128)}, u32[]{:S(2)}) copy-start(f32[2,4,24]{2,1,0:T(4,128)} %param.39) | copy-start | bytes 2308
  939.7 100.6 %copy-start.101 = (f32[2,120]{1,0:T(2,128)S(1)}, f32[2,120]{1,0:T(2,128)}, u32[]{:S(2)}) copy-start(f32[2,120]{1,0:T(2,128)} %param.40) | copy-start | bytes 2884
  939.8 100.6 %copy-start.102 = (f32[2,120]{1,0:T(2,128)S(1)}, f32[2,120]{1,0:T(2,128)}, u32[]{:S(2)}) copy-start(f32[2,120]{1,0:T(2,128)} %param.41) | copy-start | bytes 2884
  939.8 100.6 %copy-start.103 = (f32[2,120]{1,0:T(2,128)S(1)}, f32[2,120]{1,0:T(2,128)}, u32[]{:S(2)}) copy-start(f32[2,120]{1,0:T(2,128)} %param.42) | copy-start | bytes 2884
  (61 other events, 208.9 us)
Sparse Core Ops, SparseCore 0:
  122.0 7.5 reduce-scatter.20
  175.8 10.8 all-gather.7
  189.9 63.5 all-gather.9
  256.7 61.1 all-gather.11
  332.6 10.5 reduce-scatter.22
  350.5 14.2 all-gather.13
  449.6 12.8 reduce-scatter.24
  472.4 14.2 all-gather.15
  526.3 129.6 reduce-scatter.28
  661.6 127.5 reduce-scatter.18
  791.4 10.8 reduce-scatter.26
  805.1 19.5 all-reduce.10
  829.8 109.0 all-reduce.8
  940.4 12.1 all-gather.17
where the time goes:
time: 1060 us; the launch traced here: 1050 us
  waiting for transfers between devices  440 us (42%)
  blocking collectives  199 us (19%)
  matrix products  158 us (15%)
  other arithmetic  156 us (15%)
  local copies, waits for them, and re-layouts  82.1 us (8%)
  between operations  17.3 us (2%)
    unnamed x20, waiting for transfers between devices  235 us
    reduce_scatter x1, waiting for transfers between devices, body(): lax.psum_scatter(total_shrink.astype(jnp.bfloat16), 'img', scatter_dimens...  131 us
    unnamed x1, blocking collectives  77 us
    convert_element_type x2, other arithmetic, body(): act_low = gelu_exact(pre).astype(jnp.bfloat16)  69.2 us
    all_gather x1, blocking collectives, body(): lax.all_gather(norm_params.astype(jnp.bfloat16), 'img', axis=2, tiled=True)  43.6 us
    unnamed x237, local copies, waits for them, and re-layouts  40.4 us
    all_gather x1, blocking collectives, body(): lax.all_gather(filters.astype(jnp.bfloat16), 'img', axis=3, tiled=True)  38.1 us
    all_gather x1, blocking collectives, body(): lax.all_gather(mlp_bias.astype(jnp.bfloat16), 'img', axis=1, tiled=True)  37.2 us
  transfers between devices with their start and end apart: 14, of which 11 were waited for; matrix products, arithmetic and copies ran while one was open for 13% of the time, Pallas kernels for 0%

commit v1 on v0

--- a/solution.py
+++ b/solution.py
@@ -2,7 +2,11 @@
 
 import jax
 import jax.numpy as jnp
+import ml_dtypes
+import numpy as np
 from jax import lax
+from jax.experimental import pallas as pl
+from jax.experimental.pallas import tpu as pltpu
 from jax.sharding import PartitionSpec as P
 
 SIDE = 24
@@ -368,9 +372,1397 @@
     )
 
 
+LANES = 128
+TILE_ROWS = 96
+SPEC_HALF = 160
+SPEC_ROWS = 2 * SPEC_HALF
+VMEM_BYTES = 64 * 1024 * 1024
+MESH_IDS = pl.DeviceIdType.MESH
+LOG2_PEAK = -0.5 * math.log2(2.0 * math.pi)
+HALF_LOG2_E = 0.5 / math.log(2.0)
+BEND = (
+    0.7978695564437048,
+    0.03639280919444424,
+    -8.821938529071787e-05,
+    -3.660006037905966e-05,
+    1.4185332299791553e-06,
+)
+
+
+def natural_tables(parts):
+    tables = []
+    for height in (SIDE_LOW, SIDE):
+        freq_rows = np.arange(SIDE)[:, None, None, None]
+        freq_cols = np.arange(HALF)[None, :, None, None]
+        image_rows = np.arange(SIDE)[None, None, :, None]
+        columns = np.arange(SIDE)[None, None, None, :]
+        angles = ((freq_rows * image_rows + freq_cols * columns) % height) * (2.0 * np.pi / height)
+        live = (
+            (freq_rows < height)
+            & (freq_cols <= height // 2)
+            & (image_rows < height)
+            & (columns < height)
+        )
+        pair = np.stack([np.cos(angles) * live, -np.sin(angles) * live])
+        pair = pair.reshape(2, parts, SIDE * HALF // parts, SIDE * SIDE)
+        pair = np.pad(pair, ((0, 0), (0, 0), (0, SPEC_ROWS // parts - pair.shape[2]), (0, 0)))
+        tables.append(pair.reshape(2 * SPEC_ROWS, SIDE * SIDE))
+    return np.stack(tables).astype(ml_dtypes.bfloat16)
+
+
+def slot_weights():
+    weights = np.zeros((2, HALF), np.float32)
+    for group, height in enumerate((SIDE_LOW, SIDE)):
+        for freq in range(HALF):
+            weights[group, freq] = (1.0 if freq in (0, height // 2) else 2.0) / (height * height)
+    return weights
+
+
+def place(device_index):
+    return device_index // 4, device_index % 4
+
+
+def plane_peer(spot, step):
+    x, y = spot % 2, spot // 2
+    return ((y + step // 2) % 2) * 2 + (x + step % 2) % 2
+
+
+def greet(core, chip):
+    z, spot = place(chip)
+    barrier = pltpu.get_barrier_semaphore()
+    peers = [(1 - core, chip)]
+    for step in (1, 2, 3):
+        peers.append((core, z * 4 + plane_peer(spot, step)))
+        peers.append((core, ((z + step) % 4) * 4 + spot))
+    for peer in peers:
+        pl.semaphore_signal(barrier, inc=1, device_id=peer, device_id_type=MESH_IDS)
+    return barrier, len(peers)
+
+
+class Item:
+    def __init__(self, number, block, level):
+        self.number, self.block, self.level = number, block, level
+
+
+class Gather:
+    def __init__(self, core, chip, line, plane, sibling):
+        self.core, self.chip = core, chip
+        self.z, self.spot = place(chip)
+        self.line_sems, self.plane_sems, self.sibling_sems = line, plane, sibling
+
+    def level(self, step):
+        return (self.z + 4 - step) % 4
+
+    def copy(self, ref, sems, index, peer):
+        return pltpu.make_async_remote_copy(
+            src_ref=ref,
+            dst_ref=ref,
+            send_sem=sems[0].at[index],
+            recv_sem=sems[1].at[index],
+            device_id=peer,
+            device_id_type=MESH_IDS,
+        )
+
+    def line(self, item, step):
+        peer = (self.core, ((self.z + step) % 4) * 4 + self.spot)
+        index = item.number * 3 + step - 1
+        return self.copy(item.block(self.z, self.spot), self.line_sems, index, peer)
+
+    def plane(self, item, step, turn):
+        peer = (self.core, self.z * 4 + plane_peer(self.spot, turn))
+        index = item.number * 12 + step * 3 + turn - 1
+        block = item.block(self.level(step), self.spot)
+        return self.copy(block, self.plane_sems, index, peer)
+
+    def sibling(self, item, step):
+        index = item.number * 4 + step
+        peer = (1 - self.core, self.chip)
+        return self.copy(item.level(self.level(step)), self.sibling_sems, index, peer)
+
+    def begin_line(self, item):
+        for step in (1, 2, 3):
+            self.line(item, step).start()
+
+    def begin_plane(self, item):
+        for turn in (1, 2, 3):
+            self.plane(item, 0, turn).start()
+
+    def begin(self, item):
+        self.begin_line(item)
+        self.begin_plane(item)
+
+    def forward(self, item, step):
+        self.line(item, step).wait_recv()
+        for turn in (1, 2, 3):
+            self.plane(item, step, turn).start()
+
+    def share(self, item, step):
+        for turn in (1, 2, 3):
+            self.plane(item, step, turn).wait_recv()
+        self.sibling(item, step).start()
+
+    def finish(self, item):
+        for step in range(4):
+            self.sibling(item, step).wait_recv()
+
+    def drain(self, item):
+        for step in range(4):
+            if step:
+                self.line(item, step).wait_send()
+            for turn in (1, 2, 3):
+                self.plane(item, step, turn).wait_send()
+            self.sibling(item, step).wait_send()
+
+
+def add(kind, *terms):
+    total = terms[0].astype(jnp.float32)
+    for term in terms[1:]:
+        total = total + term.astype(jnp.float32)
+    return total.astype(kind)
+
+
+class Scatter:
+    def __init__(self, core, chip, number, staged, near, plane, column, line, own, sums, sems):
+        self.core, self.chip, self.number = core, chip, number
+        self.z, self.spot = place(chip)
+        self.staged, self.near, self.plane, self.column = staged, near, plane, column
+        self.line, self.own, self.sums, self.sems = line, own, sums, sems
+
+    def rows(self, core):
+        part = self.near.shape[2]
+        return pl.ds(pl.multiple_of(core * part, 16), part)
+
+    def copy(self, source, target, index, peer):
+        index += self.number * 8
+        return pltpu.make_async_remote_copy(
+            src_ref=source,
+            dst_ref=target,
+            send_sem=self.sems[0].at[index],
+            recv_sem=self.sems[1].at[index],
+            device_id=peer,
+            device_id_type=MESH_IDS,
+        )
+
+    def to_near(self):
+        other = 1 - self.core
+        source = self.staged.at[:, :, self.rows(other)]
+        return self.copy(source, self.near, 0, (other, self.chip))
+
+    def to_plane(self, turn):
+        target = plane_peer(self.spot, turn)
+        source = self.near.at[:, target]
+        return self.copy(
+            source, self.plane.at[turn - 1], turn, (self.core, self.z * 4 + target)
+        )
+
+    def to_line(self, step):
+        target = (self.z + step) % 4
+        return self.copy(
+            self.column.at[target],
+            self.line.at[step - 1],
+            3 + step,
+            (self.core, target * 4 + self.spot),
+        )
+
+    def to_sums(self):
+        return self.copy(self.own, self.sums, 7, (1 - self.core, self.chip))
+
+    def begin(self):
+        self.to_near().start()
+
+    def add_near(self):
+        self.to_near().wait_recv()
+        rows = self.rows(self.core)
+
+        def one(index, carry):
+            level, spot = index // 4, index % 4
+            mine = self.staged[level, spot, rows]
+            self.near[level, spot] = add(mine.dtype, mine, self.near[level, spot])
+            return carry
+
+        lax.fori_loop(0, 16, one, 0)
+        for turn in (1, 2, 3):
+            self.to_plane(turn).start()
+
+    def add_plane(self):
+        for turn in (1, 2, 3):
+            self.to_plane(turn).wait_recv()
+
+        def one(level, carry):
+            terms = [self.plane[turn, level] for turn in range(3)]
+            self.column[level] = add(self.column.dtype, self.near[level, self.spot], *terms)
+            return carry
+
+        lax.fori_loop(0, 4, one, 0)
+        for step in (1, 2, 3):
+            self.to_line(step).start()
+
+    def add_line(self, local_sem):
+        for step in (1, 2, 3):
+            self.to_line(step).wait_recv()
+        terms = [self.line[step] for step in range(3)]
+        total = add(jnp.float32, self.column[self.z], *terms)
+        pieces = total.shape[0] // self.own.shape[0]
+        if pieces > 1:
+            height = total.shape[0] // pieces
+            total = jnp.concatenate(
+                [total[k * height : (k + 1) * height] for k in range(pieces)], axis=1
+            )
+        self.own[...] = total
+        self.to_sums().start()
+        self.keep(local_sem).start()
+
+    def keep(self, local_sem):
+        return pltpu.make_async_copy(self.own, self.sums, local_sem)
+
+    def drain(self, local_sem, near=True):
+        self.to_sums().wait_recv()
+        if near:
+            self.to_near().wait_send()
+        for turn in (1, 2, 3):
+            self.to_plane(turn).wait_send()
+            self.to_line(turn).wait_send()
+        self.to_sums().wait_send()
+        self.keep(local_sem).wait()
+
+
+class LateScatter(Scatter):
+    def to_plane(self, turn):
+        target = plane_peer(self.spot, turn)
+        source = self.staged.at[:, target]
+        return self.copy(
+            source, self.plane.at[turn - 1], turn, (self.core, self.z * 4 + target)
+        )
+
+    def to_sibling(self):
+        return self.copy(self.own, self.near, 0, (1 - self.core, self.chip))
+
+    def begin(self):
+        for turn in (1, 2, 3):
+            self.to_plane(turn).start()
+
+    def add_plane(self):
+        for turn in (1, 2, 3):
+            self.to_plane(turn).wait_recv()
+        for level in range(4):
+            terms = [self.plane[turn, level] for turn in range(3)]
+            self.column[level] = add(self.column.dtype, self.staged[level, self.spot], *terms)
+        for step in (1, 2, 3):
+            self.to_line(step).start()
+
+    def add_line(self):
+        for step in (1, 2, 3):
+            self.to_line(step).wait_recv()
+        terms = [self.line[step] for step in range(3)]
+        self.own[...] = add(jnp.float32, self.column[self.z], *terms)
+        self.to_sibling().start()
+
+    def finish(self, total, local_sem):
+        self.to_sibling().wait()
+        for turn in (1, 2, 3):
+            self.to_plane(turn).wait_send()
+            self.to_line(turn).wait_send()
+        total[...] = self.own[...] + self.near[...]
+        copy = pltpu.make_async_copy(total, self.sums, local_sem)
+        copy.start()
+        copy.wait()
+
+
+GATHERED = LAYERS + 1
+LOCAL_SEMS = 24
+
+
+def train_kernel(
+    groups, order, keep,
+    images, cotangent, expand_own, shrink_own, filter_own, norm_own, bias_own, resample_own, factors, table_in,
+    sums_expand, sums_shrink, small_sums, out, image_grad, stash,
+    weights, smalls, maps, table, table_t, expand, filt_low, filt, norms, bias,
+    image_in, cotangent_in, normals, specs, starts, middle, grad_middle, spec,
+    inv_stds, acts, slopes, d_pre_pair, normed_pair, grad_pair,
+    grad_expand, grad_shrink, grad_filters, grad_norms, grad_bias, near, plane, column, line, own_expand, own_shrink,
+    map_rows_own, map_own, small_own, norm_tile, bias_tile,
+    early_staged, early_near, early_plane, early_column, early_line, early_own, early_total,
+    late_staged, late_near, late_plane, late_column, late_line, late_own, late_total,
+    line_send, line_recv, plane_send, plane_recv, sibling_send, sibling_recv,
+    scatter_send, scatter_recv, swap_send, swap_recv, local_sems,
+):
+    core, chip = lax.axis_index("grid"), lax.axis_index("img")
+    z, spot = place(chip)
+    other = 1 - core
+    share = image_in.shape[0]
+    rows = images.shape[1]
+    width = images.shape[3]
+    tokens = SIDE * SIDE
+    hidden = expand.shape[2]
+    owners = weights.shape[2] * weights.shape[3]
+    part = width // owners
+    quarters = hidden // width
+    chunk = hidden // 2
+    low = jnp.bfloat16
+
+    greeting = greet(core, chip)
+    image_staged = grad_middle.at[:, pl.ds(0, rows)]
+    cotangent_staged = grad_middle.at[:, pl.ds(rows, rows)]
+    image_mine = pltpu.make_async_copy(
+        images.at[pl.ds(core * share, share)],
+        image_in.at[:, pl.ds(core * rows, rows)],
+        local_sems.at[0],
+    )
+    image_stage = pltpu.make_async_copy(
+        images.at[pl.ds(other * share, share)], image_staged, local_sems.at[1]
+    )
+    cotangent_mine = pltpu.make_async_copy(
+        cotangent.at[pl.ds(core * share, share)],
+        cotangent_in.at[:, pl.ds(core * rows, rows)],
+        local_sems.at[2],
+    )
+    cotangent_stage = pltpu.make_async_copy(
+        cotangent.at[pl.ds(other * share, share)], cotangent_staged, local_sems.at[3]
+    )
+    for copy in (image_stage, image_mine, cotangent_stage, cotangent_mine):
+        copy.start()
+    norm_tile[...] = jnp.zeros_like(norm_tile)
+    small_own[...] = jnp.zeros_like(small_own)
+    bias_tile[...] = jnp.zeros_like(bias_tile)
+    bias_part = bias_own.shape[1]
+    bias_tile[:LAYERS, :bias_part] = bias_own[...]
+    shifted = lax.broadcasted_iota(jnp.int32, (LANES, 2 * LANES), 1) == (
+        lax.broadcasted_iota(jnp.int32, (LANES, 2 * LANES), 0) + chip * bias_part % LANES
+    )
+    window = dot(bias_tile[...].astype(low), shifted.astype(jnp.float32).astype(low))
+    pieces = []
+    for layer_id in range(LAYERS):
+        norm_tile[:4, :part] = norm_own[layer_id]
+        turned_norms = jnp.transpose(
+            jnp.concatenate(
+                [
+                    jnp.zeros((BASE, LANES), jnp.float32),
+                    norm_tile[...],
+                    jnp.zeros((LANES - BASE - 8, LANES), jnp.float32),
+                ],
+                axis=0,
+            )
+        )[:part]
+        small_own[:, :BASE] = filter_own[layer_id, 0]
+        pieces.append(small_own[...] + turned_norms)
+        small_own[:, :BASE] = filter_own[layer_id, 1]
+        pieces.append(small_own[...])
+    pieces += [window[:, :LANES], window[:, LANES:]]
+    pieces.append(jnp.zeros((LANES - TILE_ROWS - 16, LANES), jnp.float32))
+    block = jnp.concatenate(pieces, axis=0).astype(low)
+    small_half = LANES // 2
+
+    @pl.when(core == 0)
+    def _():
+        smalls[z, spot, 0] = block[:small_half]
+
+    @pl.when(core == 1)
+    def _():
+        smalls[z, spot, 1] = block[small_half:]
+
+    map_rows_own[...] = jnp.zeros_like(map_rows_own)
+    for freq_row in range(rows):
+        for freq_col in range(HALF):
+            slot = freq_row * HALF + freq_col
+            both = resample_own[freq_row, freq_col]
+            for group in range(2):
+                map_rows_own[group, slot : slot + 1, :BASE] = both[group : group + 1]
+    for group in range(2):
+        scaled = map_rows_own[group] * factors[group] + factors[2]
+        map_own[group] = scaled.astype(low)
+    map_rows = pl.ds(pl.multiple_of(core * SPEC_HALF, SPEC_HALF), SPEC_HALF)
+    for group in range(2):
+        maps[group, map_rows] = map_own[group]
+
+    @pl.when(core == 0)
+    def _():
+        for layer_id in range(LAYERS):
+            values = expand_own[layer_id]
+            pieces = [values[:, q * width : (q + 1) * width] for q in range(quarters)]
+            weights[0, layer_id, z, spot] = jnp.concatenate(pieces, axis=0).astype(low)
+
+    @pl.when(core == 1)
+    def _():
+        for layer_id in range(LAYERS):
+            weights[1, layer_id, z, spot] = shrink_own[layer_id].astype(low)
+
+    pl.semaphore_wait(*greeting)
+    sibling = (other, chip)
+    gather = Gather(
+        core, chip, (line_send, line_recv), (plane_send, plane_recv), (sibling_send, sibling_recv)
+    )
+    small_item = Item(
+        0,
+        lambda level, at: smalls.at[level, at, core],
+        lambda level: smalls.at[level, :, core],
+    )
+    items = [
+        Item(
+            1 + layer_id,
+            lambda level, at, layer_id=layer_id: weights.at[core, layer_id, level, at],
+            lambda level, layer_id=layer_id: weights.at[core, layer_id, level],
+        )
+        for layer_id in range(LAYERS)
+    ]
+
+    def swap(index, source, target):
+        return pltpu.make_async_remote_copy(
+            src_ref=source,
+            dst_ref=target,
+            send_sem=swap_send.at[index],
+            recv_sem=swap_recv.at[index],
+            device_id=sibling,
+            device_id_type=MESH_IDS,
+        )
+
+    half = pl.ds(core * rows, rows)
+    image_swap = swap(0, image_staged, image_in.at[:, half])
+    cotangent_swap = swap(1, cotangent_staged, cotangent_in.at[:, half])
+    map_swap = swap(2, map_own, maps.at[:, map_rows])
+    gather.begin(small_item)
+    map_swap.start()
+    image_stage.wait()
+    image_swap.start()
+    gather.begin(items[0])
+    cotangent_stage.wait()
+    cotangent_swap.start()
+
+    for group in range(2):
+
+        def order_rows(pair, carry, group=group):
+            both = jnp.concatenate(
+                [
+                    table_in[group, order[group, 2 * pair + side]].astype(jnp.float32)
+                    for side in range(2)
+                ],
+                axis=0,
+            )
+            span = pl.ds(pl.multiple_of(pair * 2 * SIDE, 16), 2 * SIDE)
+            table_t[group, span] = both.astype(low)
+            return carry
+
+        lax.fori_loop(0, SIDE // 2, order_rows, 0)
+        table[group] = jnp.transpose(table_t[group])
+
+    for step in (1, 2, 3):
+        gather.forward(small_item, step)
+    image_mine.wait()
+    image_swap.wait_recv()
+
+    def unpack_expand(layer_id):
+        def take(pair, carry):
+            level, at = pair // 2, pair % 2 * 2
+            first = weights[0, layer_id, level, at].astype(jnp.float32)
+            second = weights[0, layer_id, level, at + 1].astype(jnp.float32)
+            span = pl.ds(pl.multiple_of(2 * part * pair, 16), 2 * part)
+            for quarter in range(quarters):
+                at_rows = slice(quarter * part, (quarter + 1) * part)
+                both = jnp.concatenate([first[at_rows], second[at_rows]], axis=0)
+                expand[layer_id, span, quarter * width : (quarter + 1) * width] = both.astype(low)
+            return carry
+
+        lax.fori_loop(0, owners // 2, take, 0)
+
+    def norm_row(layer_id, index):
+        return norms[layer_id, 4 + index : 5 + index, :]
+
+    def filters_at(layer_id, group, at):
+        return [filt[layer_id, group, side, at] for side in range(2)]
+
+    def shrink_part(layer_id, piece):
+        return weights[1, layer_id, 2 * piece : 2 * piece + 2].reshape(chunk, width)
+
+    def expand_part(layer_id, piece):
+        return expand[layer_id, :, piece * chunk : (piece + 1) * chunk]
+
+    def load(source, index, at):
+        lines = slice(at.start // SIDE, at.stop // SIDE)
+        return source[index, lines].astype(jnp.float32).reshape(at.stop - at.start, width)
+
+    def store(target, index, at, values):
+        lines = slice(at.start // SIDE, at.stop // SIDE)
+        target[index, lines] = values.reshape((at.stop - at.start) // SIDE, SIDE, width).astype(low)
+
+    token_spans = spans(tokens, 2 * SIDE)
+    slot_spans = spans(SPEC_ROWS, 32)
+
+    def imag(at):
+        return slice(at.start + SPEC_ROWS, at.stop + SPEC_ROWS)
+
+    def group_of(index):
+        return groups[core * share + index]
+
+    def scale_of(index, layer_id, branch):
+        kept = keep[layer_id, branch, core * share + index].astype(jnp.float32)
+        return kept * (1.0 / (1.0 - DROP_RATES[layer_id]))
+
+    def taken(source, index):
+        return lambda at: [source[index, part] for part in (at, imag(at))]
+
+    def spectrum_of_normed(layer_id, group, at, values):
+        values = values * norm_row(layer_id, 0)
+        if at.start:
+            return values
+        height = jnp.where(group == 1, float(SIDE * SIDE), float(SIDE_LOW * SIDE_LOW))
+        first = lax.broadcasted_iota(jnp.int32, (8, 1), 0) == 0
+        top = values[:8] + jnp.where(first, height, 0.0) * norm_row(layer_id, 1)
+        return jnp.concatenate([top, values[8:]], axis=0)
+
+    def unmix(layer_id, group, take):
+        mixed_real, mixed_imag = [], []
+        for at in slot_spans:
+            real, imag_part = take(at)
+            f_real, f_imag = filters_at(layer_id, group, at)
+            mixed_real.append(real * f_real - imag_part * f_imag)
+            mixed_imag.append(real * f_imag + imag_part * f_real)
+        return dot_low(table_t[group], stack_rows(mixed_real + mixed_imag))
+
+    def mix_back(layer_id, group, scale, normal_at, take, grad_at, put):
+        low_grad = stack_rows([(grad_at(at) * scale).astype(low) for at in token_spans])
+        both = dot_low(table[group], low_grad)
+        prods, d_specs = ([], []), ([], [])
+        for at in slot_spans:
+            d_real, d_imag = both[at], both[imag(at)]
+            real, imag_part = take(at)
+            prods[0].append(d_real * real + d_imag * imag_part)
+            prods[1].append(d_imag * real - d_real * imag_part)
+            f_real, f_imag = filters_at(layer_id, group, at)
+            d_specs[0].append(d_real * f_real + d_imag * f_imag)
+            d_specs[1].append(d_imag * f_real - d_real * f_imag)
+        for side in range(2):
+            grad_filters[2 * layer_id + side] += dot_rows(stack_rows(prods[side]), maps[group])
+        d_normed = dot_low(table_t[group], stack_rows(d_specs[0] + d_specs[1]))
+        gain = norm_row(layer_id, 0)
+        sums = [jnp.zeros((8, width), jnp.float32)] * 2
+        for at in token_spans:
+            normal, inv_std = normal_at(at)
+            step = d_normed[at].astype(jnp.float32)
+            sums = [sums[0] + row_sums(step * normal), sums[1] + row_sums(step)]
+            put(at, grad_at(at) + norm_pull(step, normal, inv_std, gain))
+        grad_norms[layer_id, 0] += sums[0]
+        grad_norms[layer_id, 1] += sums[1]
+
+    def hidden_part(layer_id, piece, normed):
+        span = slice(piece * chunk, (piece + 1) * chunk)
+        pre = dot_low(normed, expand_part(layer_id, piece))
+        shift = bias[layer_id : layer_id + 1, span].astype(low)
+        pairs = [gelu_pair(pre[at] + shift) for at in spans(tokens, 32)]
+        return stack_rows([pair[0] for pair in pairs]), stack_rows([pair[1] for pair in pairs])
+
+    def normed_for_feed(layer_id, values_at):
+        gain, shift = norm_row(layer_id, 2), norm_row(layer_id, 3)
+        kept = [normalise(values_at(at)) for at in token_spans]
+        normed = stack_rows([(normal * gain + shift).astype(low) for normal, _ in kept])
+        return kept, normed
+
+    def turned_of(pair):
+        return jnp.transpose(pair[...].reshape(2 * tokens, width))
+
+    def add_expand(layer_id):
+        turned = jnp.concatenate([turned_of(normed_pair), jnp.ones((16, 2 * tokens), low)], axis=0)
+        for piece in range(3):
+            span = slice(piece * hidden // 3, (piece + 1) * hidden // 3)
+            both = dot(turned, d_pre_pair[:, :, span].reshape(2 * tokens, hidden // 3))
+            accumulate(grad_expand, span, both)
+            grad_bias[layer_id : layer_id + 1, span] += both[width : width + 1]
+
+    def add_shrink(target, turned, acts_of):
+        for piece in range(3):
+            span = slice(piece * hidden // 3, (piece + 1) * hidden // 3)
+            both = dot(turned, acts_of[:, :, span].reshape(2 * tokens, hidden // 3))
+            accumulate(target, span, both)
+
+    def branch_grad(layer_id, scale, grad_at):
+        pieces = []
+        total = jnp.zeros((8, width), jnp.float32)
+        for at in token_spans:
+            piece = (grad_at(at) * scale).astype(low)
+            total = total + row_sums(piece.astype(jnp.float32))
+            pieces.append(piece)
+        grad_bias[layer_id : layer_id + 1, hidden : hidden + width] += jnp.sum(
+            total, axis=0, keepdims=True
+        )
+        return stack_rows(pieces)
+
+    def accumulate(target, span, values):
+        for at in spans(width, 48):
+            target[at, span] += values[at]
+
+    def hidden_back(layer_id, piece, slope, grad_low, slot):
+        span = slice(piece * chunk, (piece + 1) * chunk)
+        d_act = dot_lanes(grad_low, shrink_part(layer_id, piece), low)
+        d_pre = stack_rows([d_act[at] * slope[at] for at in spans(tokens, 32)])
+        d_pre_pair[slot, :, span] = d_pre
+        return dot_lanes(d_pre, expand_part(layer_id, piece))
+
+    def feed_pull(layer_id, kept, steps, grad_at, put):
+        gain = norm_row(layer_id, 2)
+        sums = [jnp.zeros((8, width), jnp.float32)] * 2
+        for at, (normal, inv_std) in zip(token_spans, kept):
+            step = steps[0][at]
+            for more in steps[1:]:
+                step = step + more[at]
+            sums = [sums[0] + row_sums(step * normal), sums[1] + row_sums(step)]
+            put(at, grad_at(at) + norm_pull(step, normal, inv_std, gain))
+        grad_norms[layer_id, 2] += sums[0]
+        grad_norms[layer_id, 3] += sums[1]
+
+    def first_spectra(index, carry):
+        normals = [normalise(load(image_in, index, at))[0].astype(low) for at in token_spans]
+        specs[index] = dot_low(table[group_of(index)], stack_rows(normals))
+
+        @pl.when(index == 0)
+        def _():
+            for step in range(4):
+                gather.share(small_item, step)
+            gather.forward(items[0], 1)
+
+        @pl.when(index == 1)
+        def _():
+            gather.forward(items[0], 2)
+
+        @pl.when(index == 2)
+        def _():
+            gather.forward(items[0], 3)
+            gather.begin_line(items[1])
+
+        return carry
+
+    lax.fori_loop(0, share, first_spectra, 0)
+    for total in (grad_filters, grad_norms, grad_bias):
+        total[...] = jnp.zeros_like(total)
+    map_swap.wait_recv()
+    gather.finish(small_item)
+
+    bias[...] = jnp.zeros_like(bias)
+    for pair in range(owners // 2):
+        blocks = [
+            smalls[(2 * pair + side) // 4, (2 * pair + side) % 4]
+            .reshape(LANES, LANES)
+            .astype(jnp.float32)
+            for side in range(2)
+        ]
+        for index in range(2 * LAYERS):
+            span = slice(index * part, (index + 1) * part)
+            both = jnp.concatenate([block[span] for block in blocks], axis=0)
+            filt_low[index, 2 * part * pair : 2 * part * (pair + 1)] = both.astype(low)
+        for side in range(2):
+            start = (2 * pair + side) * (hidden + width) // owners // LANES * LANES
+            piece = blocks[side][TILE_ROWS : TILE_ROWS + 16]
+            bias[:, start : start + LANES] += piece[:8]
+            bias[:, start + LANES : start + 2 * LANES] += piece[8:]
+    for layer_id in range(LAYERS):
+        for group in range(2):
+            for side in range(2):
+                values = dot_lanes(maps[group], filt_low[2 * layer_id + side])
+                filt[layer_id, group, side] = values.astype(low)
+                if group == 0 and side == 0:
+                    norms[layer_id] = values[SPEC_HALF - 8 : SPEC_HALF]
+
+    def first_mix(index, carry):
+        group = group_of(index)
+        scale = scale_of(index, 0, 0)
+
+        def take(at):
+            pair = []
+            for part_at in (at, imag(at)):
+                values = specs[index, part_at].astype(jnp.float32)
+                values = spectrum_of_normed(0, group, part_at, values).astype(low)
+                specs[index, part_at] = values
+                pair.append(values)
+            return pair
+
+        mixer = unmix(0, group, take)
+        for at in token_spans:
+            starts[index, at] = load(image_in, index, at) + scale * mixer[at]
+        for step in range(4):
+
+            @pl.when(index == step)
+            def _(step=step):
+                gather.share(items[0], step)
+
+        return carry
+
+    lax.fori_loop(0, share, first_mix, 0)
+    gather.begin_plane(items[1])
+    for step in (1, 2, 3):
+        gather.forward(items[1], step)
+    gather.finish(items[0])
+    unpack_expand(0)
+
+    def stash_out(index):
+        copies = [
+            pltpu.make_async_copy(slopes.at[index % 2], stash.at[2 + index], local_sems.at[4 + index])
+        ]
+        if index < 2:
+            copies.append(
+                pltpu.make_async_copy(acts.at[index], stash.at[index], local_sems.at[20 + index])
+            )
+        return copies
+
+    def act_back(slot):
+        return pltpu.make_async_copy(stash.at[slot], acts.at[slot], local_sems.at[8 + slot])
+
+    def slope_back(index):
+        return pltpu.make_async_copy(
+            stash.at[2 + index], slopes.at[index % 2], local_sems.at[10 + index % 2]
+        )
+
+    def first_feed(index, carry):
+        slot = index % 2
+        kept, normed = normed_for_feed(0, lambda at: starts[index, at])
+        for at in range(2):
+
+            @pl.when(index == 2 + at)
+            def _(at=at):
+                for copy in stash_out(at):
+                    copy.wait()
+
+        branches = []
+        for piece in range(2):
+            span = slice(piece * chunk, (piece + 1) * chunk)
+            act, slope = hidden_part(0, piece, normed)
+            acts[slot, :, span] = act
+            slopes[slot, :, span] = slope
+            branches.append(dot(act, shrink_part(0, piece)))
+        scale = scale_of(index, 0, 1)
+        shift = bias[0:1, hidden : hidden + width]
+        for at, (normal, inv_std) in zip(token_spans, kept):
+            branch = branches[0][at] + branches[1][at] + shift
+            starts[index, at] += scale * branch
+            normals[index, at] = normal.astype(low)
+            inv_stds[index, at] = inv_std
+        for at in range(4):
+
+            @pl.when(index == at)
+            def _(at=at):
+                for copy in stash_out(at):
+                    copy.start()
+
+        for at, steps in ((1, (0,)), (2, (1,)), (3, (2, 3))):
+
+            @pl.when(index == at)
+            def _(steps=steps):
+                for step in steps:
+                    gather.share(items[1], step)
+
+        return carry
+
+    lax.fori_loop(0, share, first_feed, 0)
+    cotangent_mine.wait()
+    image_swap.wait_send()
+    cotangent_swap.wait_send()
+    cotangent_swap.wait_recv()
+
+    for total in (grad_expand, grad_shrink):
+        total[...] = jnp.zeros_like(total)
+
+    def second(turn, slot):
+        index = (2 * turn + 2) % 4 + slot
+        group = group_of(index)
+        scale = scale_of(index, 1, 0)
+        gain, shift = norm_row(1, 0), norm_row(1, 1)
+        normed = stack_rows(
+            [(normalise(starts[index, at])[0] * gain + shift).astype(low) for at in token_spans]
+        )
+        spec[index] = dot_low(table[group], normed)
+        take = taken(spec, index)
+        mixer = unmix(1, group, take)
+        for at in token_spans:
+            middle[at] = starts[index, at] + scale * mixer[at]
+        scale = scale_of(index, 1, 1)
+        kept, normed = normed_for_feed(1, lambda at: middle[at])
+        normed_pair[slot] = normed
+        grad_low = branch_grad(1, scale, lambda at: load(cotangent_in, index, at))
+        grad_pair[slot] = grad_low
+        branches, steps = [], []
+        for piece in range(2):
+            span = slice(piece * chunk, (piece + 1) * chunk)
+            act, slope = hidden_part(1, piece, normed)
+            slopes[slot, :, span] = act
+            branches.append(dot(act, shrink_part(1, piece)))
+            steps.append(hidden_back(1, piece, slope, grad_low, slot))
+        shift = bias[1:2, hidden : hidden + width]
+
+        def put_grad(at, values):
+            branch = branches[0][at] + branches[1][at] + shift
+            store(cotangent_in, index, at, middle[at] + scale * branch)
+            store(grad_middle, index, at, values)
+
+        feed_pull(1, kept, steps, lambda at: load(cotangent_in, index, at), put_grad)
+
+    def seconds(turn, carry):
+        def one(slot, inner):
+            second(turn, slot)
+            return inner
+
+        lax.fori_loop(0, 2, one, 0)
+        add_shrink(grad_shrink, turned_of(grad_pair), slopes)
+        add_expand(1)
+        return carry
+
+    gather.finish(items[1])
+    unpack_expand(1)
+    for index in (2, 3):
+        for copy in stash_out(index):
+            copy.wait()
+    lax.fori_loop(0, 2, seconds, 0)
+    for index in (2, 3):
+        slope_back(index).start()
+    gather.drain(small_item)
+    gather.drain(items[0])
+    gather.drain(items[1])
+    map_swap.wait_send()
+
+    rest = pl.ds(other * rows, rows)
+    home = pl.ds(core * share, share)
+
+    def send_home(number, source, target):
+        return (
+            swap(3 + number, source.at[:, rest], target.at[home]),
+            pltpu.make_async_copy(source.at[:, half], target.at[home], local_sems.at[12 + number]),
+        )
+
+    for copy in send_home(0, cotangent_in, out):
+        copy.start()
+
+    def stage_expand(layer_id):
+        def put(owner, carry):
+            values = grad_expand[pl.ds(pl.multiple_of(owner * part, 8), part), :]
+            pieces = [values[:, q * width : (q + 1) * width] for q in range(quarters)]
+            weights[0, layer_id, owner // 4, owner % 4] = jnp.concatenate(pieces, axis=0).astype(low)
+            return carry
+
+        lax.fori_loop(0, owners, put, 0)
+
+    def stage_shrink(grad, staged):
+        for level in range(4):
+            span = slice(level * hidden // 4, (level + 1) * hidden // 4)
+            flat = jnp.transpose(grad[:, span].astype(low))
+            staged[level] = flat.reshape(4, TILE_ROWS, width)
+
+    sems = (scatter_send, scatter_recv)
+    half_width = pl.ds(pl.multiple_of(core * hidden // 2, 128), hidden // 2)
+    half_rows = pl.ds(pl.multiple_of(core * TILE_ROWS // 2, 8), TILE_ROWS // 2)
+
+    def scatter_expand(number, layer_id):
+        return Scatter(
+            core, chip, number, weights.at[0, layer_id],
+            near.at[number], plane.at[number], column.at[number], line.at[number],
+            own_expand.at[layer_id], sums_expand.at[layer_id, :, half_width], sems,
+        )
+
+    def scatter_shrink(number, layer_id, staged):
+        return Scatter(
+            core, chip, number, staged,
+            near.at[number], plane.at[number], column.at[number], line.at[number],
+            own_shrink.at[layer_id], sums_shrink.at[layer_id, half_rows], sems,
+        )
+
+    expand_second, shrink_second = scatter_expand(0, 1), scatter_shrink(1, 1, weights.at[1, 1])
+    expand_first, shrink_first = scatter_expand(2, 0), scatter_shrink(3, 0, weights.at[0, 0])
+    tail = 2 * part
+    early_scatter = LateScatter(
+        core, chip, 4, early_staged, early_near, early_plane, early_column, early_line, early_own,
+        small_sums.at[pl.ds(tail, early_own.shape[0])], sems,
+    )
+    late_scatter = LateScatter(
+        core, chip, 5, late_staged, late_near, late_plane, late_column, late_line, late_own,
+        small_sums.at[pl.ds(0, tail)], sems,
+    )
+
+    def stage_smalls(layer_id, staged, with_bias):
+        lanes = [jnp.zeros((BASE, width), jnp.float32)]
+        lanes += [jnp.sum(grad_norms[layer_id, m], axis=0, keepdims=True) for m in range(4)]
+        lanes.append(jnp.zeros((LANES - BASE - 4, width), jnp.float32))
+        grad_filters[2 * layer_id] += jnp.transpose(jnp.concatenate(lanes, axis=0))
+        for owner in range(owners):
+            span = slice(owner * part, (owner + 1) * part)
+            start = owner * (hidden + width) // owners // LANES * LANES
+            blocks = [grad_filters[2 * layer_id + side, span] for side in range(2)]
+            if with_bias:
+                blocks.append(grad_bias[:, start : start + LANES])
+                blocks.append(grad_bias[:, start + LANES : start + 2 * LANES])
+            staged[owner // 4, owner % 4] = jnp.concatenate(blocks, axis=0).astype(low)
+
+    stage_expand(1)
+    expand_second.begin()
+    stage_shrink(grad_shrink, weights.at[1, 1])
+    shrink_second.begin()
+
+    grad_shrink[...] = jnp.zeros_like(grad_shrink)
+
+    def second_back(turn, slot):
+        index = (2 * turn + 2) % 4 + slot
+
+        def put_start(at, values):
+            starts[index, at] = values
+
+        mix_back(
+            1, group_of(index), scale_of(index, 1, 0),
+            lambda at: normalise(starts[index, at]), taken(spec, index),
+            lambda at: load(grad_middle, index, at), put_start,
+        )
+
+    def second_backs(turn, carry):
+        def one(slot, inner):
+            second_back(turn, slot)
+            return inner
+
+        lax.fori_loop(0, 2, one, 0)
+
+        @pl.when(turn == 0)
+        def _():
+            expand_second.add_near()
+            shrink_second.add_near()
+
+        @pl.when(turn == 1)
+        def _():
+            for slot in range(2):
+                act_back(slot).wait()
+
+        base = (2 * turn + 2) % 4
+        grads = [
+            branch_grad(
+                0,
+                scale_of(base + slot, 0, 1),
+                lambda at, slot=slot: starts[base + slot, at],
+            )
+            for slot in range(2)
+        ]
+        add_shrink(grad_shrink, jnp.transpose(stack_rows(grads)), acts)
+
+        @pl.when(turn == 0)
+        def _():
+            for slot in range(2):
+                act_back(slot).start()
+
+        return carry
+
+    lax.fori_loop(0, 2, second_backs, 0)
+    stage_shrink(grad_shrink, weights.at[0, 0])
+    shrink_first.begin()
+
+    grad_expand[...] = jnp.zeros_like(grad_expand)
+
+    def first_feed_back(turn, slot):
+        index = (2 * turn + 2) % 4 + slot
+        scale = scale_of(index, 0, 1)
+        gain, shift = norm_row(0, 2), norm_row(0, 3)
+        kept = [(normals[index, at].astype(jnp.float32), inv_stds[index, at]) for at in token_spans]
+        for at, (normal, _) in zip(token_spans, kept):
+            normed_pair[slot, at] = (normal * gain + shift).astype(low)
+        grad_low = stack_rows([(starts[index, at] * scale).astype(low) for at in token_spans])
+        steps = []
+        for piece in range(2):
+            span = slice(piece * chunk, (piece + 1) * chunk)
+            steps.append(hidden_back(0, piece, slopes[slot, :, span], grad_low, slot))
+
+        def put_start(at, values):
+            starts[index, at] = values
+
+        feed_pull(0, kept, steps, lambda at: starts[index, at], put_start)
+
+    def first_feed_backs(turn, carry):
+        for at in range(2):
+
+            @pl.when(turn == at)
+            def _(at=at):
+                for slot in range(2):
+                    slope_back(2 * (1 - at) + slot).wait()
+
+        def one(slot, inner):
+            first_feed_back(turn, slot)
+
+            @pl.when(turn + slot == 0)
+            def _():
+                shrink_first.add_near()
+
+            return inner
+
+        lax.fori_loop(0, 2, one, 0)
+
+        @pl.when(turn == 0)
+        def _():
+            for slot in range(2):
+                slope_back(slot).start()
+
+        add_expand(0)
+
+        @pl.when(turn == 0)
+        def _():
+            expand_second.add_plane()
+            shrink_second.add_plane()
+
+        @pl.when(turn == 1)
+        def _():
+            shrink_first.add_plane()
+
+        return carry
+
+    lax.fori_loop(0, 2, first_feed_backs, 0)
+    shrink_first.to_near().wait_send()
+    stage_expand(0)
+    expand_first.begin()
+    stage_smalls(1, early_staged, True)
+    early_scatter.begin()
+
+    def first_mix_back(index, carry):
+        def take(at):
+            return [specs[index, part_at] for part_at in (at, imag(at))]
+
+        def put_image(at, values):
+            store(image_in, index, at, values)
+
+        mix_back(
+            0, group_of(index), scale_of(index, 0, 0),
+            lambda at: normalise(load(image_in, index, at)), take,
+            lambda at: starts[index, at], put_image,
+        )
+
+        @pl.when(index == 0)
+        def _():
+            expand_first.add_near()
+
+        @pl.when(index == 1)
+        def _():
+            expand_second.add_line(local_sems.at[14])
+            shrink_second.add_line(local_sems.at[15])
+
+        @pl.when(index == 2)
+        def _():
+            early_scatter.add_plane()
+
+        @pl.when(index == 3)
+        def _():
+            early_scatter.add_line()
+
+        return carry
+
+    lax.fori_loop(0, share, first_mix_back, 0)
+    for copy in send_home(1, image_in, image_grad):
+        copy.start()
+
+    stage_smalls(0, late_staged, False)
+    late_scatter.begin()
+    shrink_first.add_line(local_sems.at[16])
+    expand_first.add_plane()
+    late_scatter.add_plane()
+    expand_first.add_line(local_sems.at[17])
+    late_scatter.add_line()
+    for number, (source, target) in enumerate(((cotangent_in, out), (image_in, image_grad))):
+        for copy in send_home(number, source, target):
+            copy.wait()
+    expand_second.drain(local_sems.at[14])
+    shrink_second.drain(local_sems.at[15])
+    shrink_first.drain(local_sems.at[16], near=False)
+    expand_first.drain(local_sems.at[17])
+    early_scatter.finish(early_total, local_sems.at[18])
+    late_scatter.finish(late_total, local_sems.at[19])
+
+
+def train(
+    groups, order, keep, images, cotangent, expand, shrink, filters, norms, biases, maps, factors, table
+):
+    count, rows, _, width = images.shape
+    share = count // 2
+    tokens = SIDE * SIDE
+    hidden = expand.shape[2]
+    low, full = jnp.bfloat16, jnp.float32
+    block = (TILE_ROWS, width)
+    half = (TILE_ROWS // 2, width)
+    small = (LANES // 2, LANES)
+    anywhere = pl.BlockSpec(memory_space=pl.ANY)
+    inside = pl.BlockSpec(memory_space=pltpu.VMEM)
+    scalar = pl.BlockSpec(memory_space=pltpu.SMEM)
+    whole = (share, SIDE, SIDE, width)
+    sems = pltpu.SemaphoreType.DMA
+
+    def late_buffers(height):
+        small = (height, LANES)
+        return (
+            pltpu.VMEM((4, 4) + small, low),
+            pltpu.VMEM(small, full),
+            pltpu.VMEM((3, 4) + small, low),
+            pltpu.VMEM((4,) + small, low),
+            pltpu.VMEM((3,) + small, low),
+            pltpu.VMEM(small, full),
+            pltpu.VMEM(small, full),
+        )
+
+    return pl.pallas_call(
+        train_kernel,
+        out_shape=(
+            jax.ShapeDtypeStruct(expand.shape, full),
+            jax.ShapeDtypeStruct(shrink.shape, full),
+            jax.ShapeDtypeStruct((TILE_ROWS + 16, LANES), full),
+            jax.ShapeDtypeStruct(images.shape, low),
+            jax.ShapeDtypeStruct(images.shape, low),
+            jax.ShapeDtypeStruct((6, tokens, hidden), low),
+        ),
+        in_specs=[scalar] * 3 + [anywhere] * 2 + [inside] * 8,
+        out_specs=[anywhere] * 6,
+        scratch_shapes=[
+            pltpu.VMEM((2, LAYERS, 4, 4) + block, low),
+            pltpu.VMEM((4, 4, 2) + small, low),
+            pltpu.VMEM((2, SPEC_ROWS, LANES), low),
+            pltpu.VMEM((2, 2 * SPEC_ROWS, tokens), low),
+            pltpu.VMEM((2, tokens, 2 * SPEC_ROWS), low),
+            pltpu.VMEM((LAYERS, width, hidden), low),
+            pltpu.VMEM((2 * LAYERS, width, LANES), low),
+            pltpu.VMEM((LAYERS, 2, 2, SPEC_ROWS, width), low),
+            pltpu.VMEM((LAYERS, 8, width), full),
+            pltpu.VMEM((8, 2048), full),
+            pltpu.VMEM(whole, low),
+            pltpu.VMEM(whole, low),
+            pltpu.VMEM((share, tokens, width), low),
+            pltpu.VMEM((share, 2 * SPEC_ROWS, width), low),
+            pltpu.VMEM((share, tokens, width), full),
+            pltpu.VMEM((tokens, width), full),
+            pltpu.VMEM(whole, low),
+            pltpu.VMEM((share, 2 * SPEC_ROWS, width), low),
+            pltpu.VMEM((share, tokens, 1), full),
+            pltpu.VMEM((2, tokens, hidden), low),
+            pltpu.VMEM((2, tokens, hidden), low),
+            pltpu.VMEM((2, tokens, hidden), low),
+            pltpu.VMEM((2, tokens, width), low),
+            pltpu.VMEM((2, tokens, width), low),
+            pltpu.VMEM((width, hidden), full),
+            pltpu.VMEM((width, hidden), full),
+            pltpu.VMEM((2 * LAYERS, width, LANES), full),
+            pltpu.VMEM((LAYERS, 4, 8, width), full),
+            pltpu.VMEM((8, 2048), full),
+            pltpu.VMEM((2 * LAYERS, 4, 4) + half, low),
+            pltpu.VMEM((2 * LAYERS, 3, 4) + half, low),
+            pltpu.VMEM((2 * LAYERS, 4) + half, low),
+            pltpu.VMEM((2 * LAYERS, 3) + half, low),
+            pltpu.VMEM((LAYERS, expand.shape[1], hidden // 2), full),
+            pltpu.VMEM((LAYERS,) + half, full),
+            pltpu.VMEM((2, SPEC_HALF, LANES), full),
+            pltpu.VMEM((2, SPEC_HALF, LANES), low),
+            pltpu.VMEM((filters.shape[2], LANES), full),
+            pltpu.VMEM((8, LANES), full),
+            pltpu.VMEM((8, LANES), full),
+            *late_buffers(TILE_ROWS + 16 - 2 * expand.shape[1]),
+            *late_buffers(2 * expand.shape[1]),
+            sems((GATHERED * 3,)),
+            sems((GATHERED * 3,)),
+            sems((GATHERED * 12,)),
+            sems((GATHERED * 12,)),
+            sems((GATHERED * 4,)),
+            sems((GATHERED * 4,)),
+            sems((48,)),
+            sems((48,)),
+            sems((5,)),
+            sems((5,)),
+            sems((LOCAL_SEMS,)),
+        ],
+        compiler_params=pltpu.CompilerParams(
+            collective_id=0, has_side_effects=True, vmem_limit_bytes=VMEM_BYTES
+        ),
+    )(
+        groups, order, keep, images, cotangent, expand, shrink, filters, norms, biases, maps, factors, table
+    )
+
+
+def gelu_pair(values):
+    square = values * values
+    curve = BEND[4] * square + BEND[3]
+    for coefficient in (BEND[2], BEND[1], BEND[0]):
+        curve = curve * square + coefficient
+    below = 0.5 * jnp.tanh(values * curve) + 0.5
+    bell = jnp.exp2(square * (-HALF_LOG2_E) + LOG2_PEAK)
+    return values * below, below + values * bell
+
+
+def normalise(values):
+    centred = values - jnp.mean(values, axis=-1, keepdims=True)
+    variance = jnp.mean(centred * centred, axis=-1, keepdims=True)
+    inv_std = lax.rsqrt(variance + NORM_EPS)
+    return centred * inv_std, inv_std
+
+
+def norm_pull(grad_out, normal, inv_std, gain):
+    scaled = grad_out * gain
+    return inv_std * (
+        scaled
+        - jnp.mean(scaled, axis=-1, keepdims=True)
+        - normal * jnp.mean(scaled * normal, axis=-1, keepdims=True)
+    )
+
+
+def spans(count, size):
+    return [slice(start, start + size) for start in range(0, count, size)]
+
+
+def stack_rows(pieces):
+    return jnp.concatenate(pieces, axis=0)
+
+
+def row_sums(values):
+    return jnp.sum(values.reshape(values.shape[0] // 8, 8, values.shape[1]), axis=0)
+
+
+def dot(left, right):
+    return jnp.dot(left, right, preferred_element_type=jnp.float32)
+
+
+def dot_low(left, right):
+    return dot(left, right).astype(jnp.bfloat16)
+
+
+def dot_lanes(left, right, kind=jnp.float32):
+    return lax.dot_general(
+        left, right, (((1,), (1,)), ((), ())), preferred_element_type=jnp.float32
+    ).astype(kind)
+
+
+def dot_rows(left, right):
+    return lax.dot_general(
+        left, right, (((0,), (0,)), ((), ())), preferred_element_type=jnp.float32
+    )
+
+
+def update_kernel(*refs):
+    owner = lax.axis_index("img")
+    sources, targets = refs[:20], refs[20:37]
+    smalls, output, image_grad = sources[17:20]
+    step = pl.program_id(0)
+    targets[15][...] = output[...]
+
+    def apply(index, grad, at=(Ellipsis,)):
+        values = [ref[at] for ref in sources[3 * index : 3 * index + 3]]
+        results = adamw(*values, grad, LEARN_RATES[index], WEIGHT_DECAYS[index])
+        for target, result in zip(targets[3 * index : 3 * index + 3], results):
+            target[at] = result
+
+    apply(1, sources[15][...])
+    apply(2, sources[16][...])
+    targets[16][...] = image_grad[...].astype(targets[16].dtype)
+
+    @pl.when(step == 0)
+    def _():
+        part = sources[0].shape[2]
+        bias_part = sources[12].shape[1]
+        for layer_id in range(LAYERS):
+            for side in range(2):
+                start = (2 * layer_id + side) * part
+                apply(0, smalls[start : start + part, :BASE], (layer_id, side))
+            start = 2 * layer_id * part
+            block = jnp.concatenate(
+                [smalls[start : start + part], jnp.zeros((LANES - part, LANES), jnp.float32)], axis=0
+            )
+            apply(3, jnp.transpose(block)[BASE : BASE + 4, :part], (layer_id,))
+        window = jnp.concatenate(
+            [smalls[TILE_ROWS : TILE_ROWS + 8], smalls[TILE_ROWS + 8 : TILE_ROWS + 16]], axis=1
+        )
+        offset = owner * bias_part % LANES
+        window = pltpu.roll(window, 2 * LANES - offset, 1)
+        apply(4, window[:LAYERS, :bias_part])
+
+
+def update(params, sum_expand, sum_shrink, smalls, output, image_grad):
+    steps = 4
+
+    def along(array, axis):
+        block = list(array.shape)
+        block[axis] //= steps
+        return pl.BlockSpec(
+            tuple(block), lambda step: tuple(step if k == axis else 0 for k in range(len(block)))
+        )
+
+    def whole(array):
+        return pl.BlockSpec(array.shape, lambda step: (0,) * array.ndim)
+
+    param_specs = []
+    for index, array in enumerate(params):
+        kind = index // 3
+        param_specs.append(along(array, 3 - kind) if kind in (1, 2) else whole(array))
+    image_specs = [along(output, 0), along(image_grad, 0)]
+    return pl.pallas_call(
+        update_kernel,
+        grid=(steps,),
+        in_specs=param_specs
+        + [along(sum_expand, 2), along(sum_shrink, 1), whole(smalls)]
+        + image_specs,
+        out_specs=param_specs + image_specs,
+        out_shape=[jax.ShapeDtypeStruct(array.shape, jnp.float32) for array in params]
+        + [
+            jax.ShapeDtypeStruct(output.shape, output.dtype),
+            jax.ShapeDtypeStruct(image_grad.shape, jnp.float32),
+        ],
+        compiler_params=pltpu.CompilerParams(vmem_limit_bytes=VMEM_BYTES),
+    )(*params, sum_expand, sum_shrink, smalls, output, image_grad)
+
+
+def whole_image_body(
+    images,
+    cotangent,
+    image_group,
+    row_order,
+    keep_mask,
+    resample,
+    filters,
+    filters_first,
+    filters_second,
+    expand,
+    expand_first,
+    expand_second,
+    shrink,
+    shrink_first,
+    shrink_second,
+    norm_params,
+    norm_first,
+    norm_second,
+    mlp_bias,
+    bias_first,
+    bias_second,
+):
+    count, rows, _, width = images.shape
+    low = jnp.bfloat16
+    factors = np.zeros((3, SPEC_HALF, LANES), np.float32)
+    factors[:2, : rows * HALF] = np.tile(slot_weights(), (1, rows))[:, :, None]
+    for index in range(4):
+        factors[2, rows * HALF + index, BASE + index] = 1.0
+    table = natural_tables(2).transpose(0, 2, 1).reshape(2, SIDE, SIDE, 2 * SPEC_ROWS)
+    filter_group = [
+        array.transpose(0, 2, 3, 1) for array in (filters, filters_first, filters_second)
+    ]
+    sum_expand, sum_shrink, small_sums, output, image_grad, _ = train(
+        image_group,
+        row_order,
+        keep_mask.transpose(1, 2, 0),
+        images,
+        cotangent,
+        expand,
+        shrink,
+        filter_group[0],
+        norm_params,
+        mlp_bias,
+        resample.transpose(1, 2, 0, 3),
+        jnp.asarray(factors),
+        jnp.asarray(table),
+    )
+    results = update(
+        filter_group
+        + [expand, expand_first, expand_second]
+        + [shrink, shrink_first, shrink_second]
+        + [norm_params, norm_first, norm_second]
+        + [mlp_bias, bias_first, bias_second],
+        sum_expand,
+        sum_shrink,
+        small_sums,
+        output,
+        image_grad,
+    )
+    new_filters = [array.transpose(0, 3, 1, 2) for array in results[:3]]
+    return (results[15], results[16], *new_filters, *results[3:15])
+
+
 def solution(mesh):
+    paired = mesh.shape["grid"] == 2 and mesh.shape["img"] == 16
     return jax.shard_map(
-        body,
+        whole_image_body if paired else body,
         mesh=mesh,
         in_specs=(
             P("img", "grid", None, None),

time: 1060 us -> 133 us (0.13)
  waiting for transfers between devices: 440 us -> 0 us
  blocking collectives: 199 us -> 0 us
  matrix products: 158 us -> 0 us
  other arithmetic: 156 us -> 0 us
  Pallas kernels: 0 us -> 132 us
  local copies, waits for them, and re-layouts: 82.1 us -> 0 us
  between operations: 17.3 us -> 0.84 us
    unnamed x20 -> x0, waiting for transfers between devices: 235 us -> none
    dot_general x26 -> x0, matrix products: 158 us -> none  [the longest x2 35.4 us: body(): jnp.einsum('itd,fd->itf', grad_branch, shrink_all[layer_id], preferred_el...]
    pallas_call x0 -> x2, Pallas kernels: none -> 132 us  [the longest x1 125 us: train(): pl.pallas_call(train_kernel, out_shape=(jax.ShapeDtypeStruct(expand.shape...]
    reduce_scatter x1 -> x0, waiting for transfers between devices: 131 us -> none  [body(): lax.psum_scatter(total_shrink.astype(jnp.bfloat16), 'img', scatter_dimens...]
    all_gather x3 -> x0, blocking collectives: 119 us -> none  [the longest x1 43.6 us: body(): lax.all_gather(norm_params.astype(jnp.bfloat16), 'img', axis=2, tiled=True)]
    unnamed x1 -> x0, blocking collectives: 77 us -> none
    convert_element_type x8 -> x0, other arithmetic: 73.4 us -> none  [the longest x2 69.2 us: body(): act_low = gelu_exact(pre).astype(jnp.bfloat16)]
    all_gather x6 -> x0, waiting for transfers between devices: 73.1 us -> none  [the longest x1 29.7 us: body(): lax.all_gather(expand.astype(jnp.bfloat16), 'img', axis=1, tiled=True)]
  transfers between devices with their start and end apart: 14 -> 0, of which waited for: 11 -> 0; matrix products, arithmetic and copies ran while one was open for 13% -> 0% of each run, Pallas kernels for 0% -> 0%
where the time goes in v1:
time: 133 us
  Pallas kernels  132 us (99%)
    pallas_call x1, Pallas kernels, train(): pl.pallas_call(train_kernel, out_shape=(jax.ShapeDtypeStruct(expand.shape...  125 us
    pallas_call x1, Pallas kernels, update(): pl.pallas_call(update_kernel, grid=(steps,), in_specs=param_specs + [alon...  6.65 us

profile of v1, /device:TPU:0, one launch (start us, length us, event | category | flops | bytes accessed | tf_op | source)
XLA Modules:
  0.0 132.8 jit_solution(17917644828554541752)
XLA Ops:
  0.7 125.3 %shard_map.350 = (f32[2,24,1536]{2,1,0:T(8,128)}, f32[2,96,384]{2,1,0:T(8,128)}, f32[112,128]{1,0:T(8,128)}, bf16[8,12,24,384]{3,2,1,0:T(8,128)(2,1)}, bf16[8,12...) custom-call(s32[8]{0:T(128)} %groups.1, s32[2,24]{1,0:T(2,128)} %order.1, s32[2,2,8]{2,1,0:T(2,128)} %bitcast.13, ...), custom_call_target="tpu_custom_call" | custom-call | tf_op jit(solution)/shard_map/pallas_call | solution.py:1493
  125.9 6.6 %shard_map.351 = (f32[2,2,24,112]{3,2,1,0:T(8,128)}, f32[2,2,24,112]{3,2,1,0:T(8,128)}, f32[2,2,24,112]{3,2,1,0:T(8,128)}, f32[2,24,1536]{2,1,0:T(8,128)}, f32[2...) custom-call(f32[2,2,24,112]{3,2,1,0:T(8,128)} %bitcast.9, ...), custom_call_target="tpu_custom_call" | custom-call | tf_op jit(solution)/shard_map/pallas_call | solution.py:1682
